TPU v7x, 256 devices: a whole 4x4x8 slice. The times are simulated.
256 devices in a mesh: dp: 4 (over x), tiles: 64 (over z, y, core).
Axes of the slice: x: 4, y: 4, z: 8, core: 2. Of those that a mesh axis runs over, the one named last changes fastest.
Arguments:
- fields: bfloat16 [4, 256, 16, 3072], P('dp', 'tiles'), may hold values from -6 to 6
- ocean_mask: int32 [256, 16, 16], P('tiles'), may hold values 0 or 1
- neighbours: int32 [256, 8], P('tiles'), may hold values from -1 to 255, as said below
- dw_kernel: float32 [49, 192], replicated, may hold values from -0.875 to 0.875
- ln_gain: float32 [192], replicated, may hold values from 0.5 to 2
- ln_bias: float32 [192], replicated, may hold values from -3 to 3
- w_in: bfloat16 [192, 768], replicated, may hold values from -0.4375 to 0.4375
- b_in: float32 [768], replicated, may hold values from -3 to 3
- w_out: bfloat16 [768, 192], replicated, may hold values from -0.21875 to 0.21875
- layer_scale: float32 [192], replicated, may hold values from 0.3 to 1.5
- cotangent: bfloat16 [4, 256, 16, 3072], P('dp', 'tiles'), may hold values from -6 to 6
Outputs:
- block_out: bfloat16 [4, 256, 16, 3072], P('dp', 'tiles')
- field_grad: bfloat16 [4, 256, 16, 3072], P('dp', 'tiles')
- grad_kernel: float32 [49, 192], replicated
- grad_gain: float32 [192], replicated
- grad_shift: float32 [192], replicated
- grad_in: float32 [192, 768], replicated
- grad_bias: float32 [768], replicated
- grad_out: float32 [768, 192], replicated
- grad_scale: float32 [192], replicated
Inputs may be any that keep to these rules, and one draw needn't show every extreme that they name: `neighbours`: row s lists the slots of the tiles around tile s in the order of the steps, -1 where that tile is land or off the slab; the relation is symmetric. Slots number the ocean tiles row by row, so the neighbour at (0,-1) holds slot s - 1, the one at (0,1) slot s + 1, those with dy = -1 lower and those with dy = 1 higher slots, all within 9 of s.
All inputs are finite; a program needn't handle non-finite values. No bound on the sum of `ocean_mask` on one device may be relied on, other than what follows from the above.
Results may differ from a plain program's by a relative error of at most 0.007.
Values may be sent and summed in bfloat16 or wider, within the bound.
No kernel may reach another device: no remote copies, remote signals or barrier semaphores. Data moves between devices by JAX's collectives and lax.ppermute only.
A program may use at most 64 MiB of HBM per device.

v0:
```python
import math

import jax
import jax.numpy as jnp
from jax import lax
from jax.sharding import PartitionSpec as P

KS = 7
REACH = 3


RIM_FOR_DIRECTION = (0, 0, 0, 2, 3, 1, 1, 1)
INV_SQRT2 = 0.7071067811865476
INV_SQRT_2PI = 0.3989422804014327


def shifted_2(block, axis, distance):
    devices = range(lax.axis_size(axis))
    route = [(i - distance, i) for i in devices if i - distance in devices]
    return lax.ppermute(block, axis, route)


def border_rims(tile_set):
    leading = tile_set.shape[:-3]
    tile_len = tile_set.shape[-3]
    width = tile_len * tile_set.shape[-1]
    top_rows = tile_set[..., tile_len - 3 :, :, :].reshape(leading + (3, width))
    bottom_rows = tile_set[..., :3, :, :].reshape(leading + (3, width))
    right_cols = jnp.swapaxes(tile_set[..., :, tile_len - 3 :, :], -3, -2).reshape(
        leading + (3, width)
    )
    left_cols = jnp.swapaxes(tile_set[..., :, :3, :], -3, -2).reshape(leading + (3, width))
    return jnp.stack([top_rows, bottom_rows, right_cols, left_cols], axis=-3)


def assemble(tile_set, picked):
    leading = tile_set.shape[:-3]
    tile_len = tile_set.shape[-3]
    channels = tile_set.shape[-1]
    pieces = picked.reshape(leading + (8, 3, tile_len, channels))
    south = jnp.concatenate(
        [pieces[..., 0, :, tile_len - 3 :, :], pieces[..., 1, :, :, :], pieces[..., 2, :, :3, :]],
        axis=-2,
    )
    west_side = jnp.swapaxes(pieces[..., 3, :, :, :], -3, -2)
    east_side = jnp.swapaxes(pieces[..., 4, :, :, :], -3, -2)
    middle = jnp.concatenate([west_side, tile_set, east_side], axis=-2)
    north = jnp.concatenate(
        [pieces[..., 5, :, tile_len - 3 :, :], pieces[..., 6, :, :, :], pieces[..., 7, :, :3, :]],
        axis=-2,
    )
    return jnp.concatenate([south, middle, north], axis=-3)


def extend_tiles(tile_set, neighbours):
    samples = tile_set.shape[0]
    per_dev = tile_set.shape[1]
    borders = border_rims(tile_set)
    width = borders.shape[-1]
    from_below = []
    from_above = []
    for offset in range(1, REACH + 1):
        from_below.append(shifted_2(borders, "tiles", offset))
        from_above.append(shifted_2(borders, "tiles", -offset))
    stacked = jnp.concatenate(
        [borders] + from_below + from_above + [jnp.zeros_like(borders[:, :1])], axis=1
    )
    flat_rims = stacked.reshape(samples, -1, 3, width)
    own_index = lax.axis_index("tiles")
    owner_dev = neighbours // per_dev
    distance = owner_dev - own_index
    source_block = jnp.where(distance < 0, -distance, jnp.where(distance > 0, REACH + distance, 0))
    entries = source_block * per_dev + neighbours % per_dev
    entries = jnp.where(neighbours < 0, (2 * REACH + 1) * per_dev, entries)
    lookup = entries * 4 + jnp.array(RIM_FOR_DIRECTION, dtype=jnp.int32)
    picked = jnp.take(flat_rims, lookup.reshape(-1), axis=1).reshape(samples, per_dev, 8, 3, width)
    return assemble(tile_set, picked)


def depthwise(padded, kernel, tile_len):
    total = jnp.zeros(padded.shape[:-3] + (tile_len, tile_len, padded.shape[-1]), jnp.float32)
    for row_tap in range(KS):
        for col_tap in range(KS):
            window = padded[..., row_tap : row_tap + tile_len, col_tap : col_tap + tile_len, :]
            total = total + window.astype(jnp.float32) * kernel[KS * row_tap + col_tap]
    return total


def kernel_grad(padded, back_conv, tile_len):
    back_values = back_conv.astype(jnp.float32)
    axes_all = tuple(range(back_values.ndim - 1))
    taps = []
    for row_tap in range(KS):
        for col_tap in range(KS):
            window = padded[..., row_tap : row_tap + tile_len, col_tap : col_tap + tile_len, :]
            taps.append(jnp.sum(window.astype(jnp.float32) * back_values, axis=axes_all))
    return jnp.stack(taps, axis=0)


def contract_rows(left_side, right_side):
    return lax.dot_general(
        left_side, right_side, (((0,), (0,)), ((), ())), preferred_element_type=jnp.float32
    )


def contract_cols(left_side, right_side):
    return lax.dot_general(
        left_side, right_side, (((1,), (1,)), ((), ())), preferred_element_type=jnp.float32
    )


def shards(
    fields,
    ocean_mask,
    neighbours,
    dw_kernel,
    ln_gain,
    ln_bias,
    w_in,
    b_in,
    w_out,
    layer_scale,
    cotangent,
):
    samples, per_dev, tile_len, width = fields.shape
    channels = dw_kernel.shape[1]
    tile_set = fields.reshape(samples, per_dev, tile_len, tile_len, channels)
    keep_cells = (ocean_mask > 0)[None, :, :, :, None]
    keep_float = keep_cells.astype(jnp.float32)
    masked = jnp.where(keep_cells, tile_set, jnp.zeros_like(tile_set))
    padded = extend_tiles(masked, neighbours)
    conv_out = depthwise(padded, dw_kernel, tile_len)
    seed_tiles = cotangent.reshape(tile_set.shape).astype(jnp.float32) * keep_float
    cell_count = (
        samples * per_dev * tile_len * tile_len * lax.axis_size("dp") * lax.axis_size("tiles")
    )
    factor = 1.0 / math.sqrt(cell_count)
    conv_rows = conv_out.reshape(-1, channels)
    seed_rows = seed_tiles.reshape(-1, channels)
    keep_rows = keep_float.reshape(-1, 1)
    mean_val = jnp.mean(conv_rows, axis=-1, keepdims=True)
    centred = conv_rows - mean_val
    inv_std = lax.rsqrt(jnp.mean(centred * centred, axis=-1, keepdims=True) + 1e-06)
    normed = centred * inv_std
    shifted = (normed * ln_gain + ln_bias).astype(jnp.bfloat16)
    preact = jnp.dot(shifted, w_in, preferred_element_type=jnp.float32) + b_in
    gelu_cdf = 0.5 * (1.0 + jax.scipy.special.erf(preact * INV_SQRT2))
    hidden = (preact * gelu_cdf).astype(jnp.bfloat16)
    branch = jnp.dot(hidden, w_out, preferred_element_type=jnp.float32)
    result = (
        keep_rows * (masked.reshape(-1, channels).astype(jnp.float32) + layer_scale * branch)
    ).astype(jnp.bfloat16)
    grad_scale_part = jnp.sum(seed_rows * branch, axis=0) * factor
    back_branch = (seed_rows * layer_scale).astype(jnp.bfloat16)
    grad_out_part = contract_rows(hidden, back_branch) * factor
    back_hidden = contract_cols(back_branch, w_out)
    density = jnp.exp(-0.5 * preact * preact) * INV_SQRT_2PI
    back_pre = (back_hidden * (gelu_cdf + preact * density)).astype(jnp.bfloat16)
    grad_bias_part = jnp.sum(back_pre.astype(jnp.float32), axis=0) * factor
    grad_in_part = contract_rows(shifted, back_pre) * factor
    back_shift = contract_cols(back_pre, w_in)
    grad_gain_part = jnp.sum(back_shift * normed, axis=0) * factor
    grad_shift_part = jnp.sum(back_shift, axis=0) * factor
    scaled = back_shift * ln_gain
    back_conv = (
        inv_std
        * (
            scaled
            - jnp.mean(scaled, axis=-1, keepdims=True)
            - normed * jnp.mean(scaled * normed, axis=-1, keepdims=True)
        )
    ).astype(jnp.bfloat16)
    back_conv = back_conv.reshape(tile_set.shape)
    back_padded = extend_tiles(back_conv, neighbours)
    field_grad = (
        keep_float * (seed_tiles + depthwise(back_padded, dw_kernel[::-1], tile_len))
    ).astype(jnp.bfloat16)
    grad_kernel_part = kernel_grad(padded, back_conv, tile_len) * factor
    grad_kernel, grad_gain, grad_shift, grad_in, grad_bias, grad_out, grad_scale = lax.psum(
        (
            grad_kernel_part,
            grad_gain_part,
            grad_shift_part,
            grad_in_part,
            grad_bias_part,
            grad_out_part,
            grad_scale_part,
        ),
        ("dp", "tiles"),
    )
    return (
        result.reshape(fields.shape),
        field_grad.reshape(fields.shape),
        grad_kernel,
        grad_gain,
        grad_shift,
        grad_in,
        grad_bias,
        grad_out,
        grad_scale,
    )


def solution(mesh):
    in_specs = (
        P("dp", "tiles", None, None),
        P("tiles", None, None),
        P("tiles", None),
        P(),
        P(),
        P(),
        P(),
        P(),
        P(),
        P(),
        P("dp", "tiles", None, None),
    )
    out_specs = (
        P("dp", "tiles", None, None),
        P("dp", "tiles", None, None),
        P(),
        P(),
        P(),
        P(),
        P(),
        P(),
        P(),
    )
    return jax.shard_map(shards, mesh=mesh, in_specs=in_specs, out_specs=out_specs, check_vma=False)
```

profile of v0, /device:TPU:1, one launch (start us, length us, event | category | flops | bytes accessed | tf_op | source)
XLA Modules:
  0.0 414.2 jit_solution(12799582367973072168)
XLA Ops:
  8.0 1.6 reshape.504
  13.4 4.6 %collective-permute-start = (bf16[1,4,4,3,3072]{4,1,3,2,0:T(4,128)(2,1)}, bf16[1,4,4,3,3072]{4,1,3,2,0:T(4,128)(2,1)}, u32[]{:S(2)}, u32[]{:S(2)}) collective-permute-start(bf16[1,4,4,3,3072]{4,1,3,2,0:T(4,128)(2,1)} %constant_dynamic-update-slice_fusion), channel_id=1, source_target_pairs={{0,1},{1,2},{2,3},{3,4},{4,5},{5,6},{6,7},{7,8},{8,9},{9,10},{10,1... | collective-permute-start | bytes 884744 | tf_op jit(solution)/shard_map/ppermute | solution.py:20
  18.0 3.9 collective-permute-start.1
  21.9 3.5 collective-permute-start.2
  25.4 1.9 collective-permute-start.3
  31.5 1.6 reshape.513
  37.5 1.8 collective-permute-start.5
  40.0 8.4 %collective-permute-done.5 = bf16[1,4,4,3,3072]{4,1,3,2,0:T(4,128)(2,1)S(1)} collective-permute-done((bf16[1,4,4,3,3072]{4,1,3,2,0:T(4,128)(2,1)}, bf16[1,4,4,3,3072]{4,1,3,2,0:T(4,128)(2,1)S(1)}, u32[]{:S(2)}, u32[]{:S(2)}) %collective-permute-start.5) | collective-permute-done | bytes 294944 | tf_op jit(solution)/shard_map/ppermute | solution.py:20
  48.5 13.1 %concatenate.138 = bf16[1,29,4,3,3072]{4,1,3,2,0:T(8,128)(2,1)} concatenate(bf16[1,4,4,3,3072]{4,1,3,2,0:T(4,128)(2,1)} %constant_dynamic-update-slice_fusion, bf16[1,4,4,3,3072]{4,1,3,2,0:T(4,128)(2,1)} %collective-permute-done, bf16[1,4,4,3,3072]{4,1,3,2,0:T(4,128)(2,1)} %collective-permute-done.1, bf16[1,4,4,3,3072]{4,1,3,2,0:T(4,128)(2,1)} %collective-permute-done.2, ...), dimensions={1} | concatenate | bytes 4276224 | tf_op jit(solution)/shard_map/concatenate | solution.py:65
  61.6 5.1 %copy.133 = bf16[1,29,4,3,3072]{4,3,2,1,0:T(4,128)(2,1)} copy(bf16[1,29,4,3,3072]{4,1,3,2,0:T(8,128)(2,1)} %concatenate.138) | data formatting | bytes 4276224 | tf_op jit(solution)/shard_map/reshape | solution.py:68
  66.7 3.0 gather_fusion
  72.9 9.4 %fusion.143 = (f32[4,16,16]{2,1,0:T(8,128)S(1)}, f32[1,4,16,16,192]{4,3,2,1,0:T(8,128)}) fusion(f32[192]{0:T(256)S(1)} %bitcast.305, bf16[1,4,19,22,192]{4,3,2,1,0:T(8,128)(2,1)S(1)} %get-tuple-element.98, f32[192]{0:T(256)S(1)} %bitcast.307, f32[192]{0:T(256)S(1)} %bitcast.311, f32[192]{0:T(256)S(1)} %bitcast.313, f32[192]{0:T(256)S(1)} %bitcast.315, ...), kind=kLoop, calls=%fused_computation.336 | loop fusion | flops 32439296 | bytes 17883904 | tf_op jit(solution)/shard_map/reduce_sum | solution.py:141
  82.4 1.6 multiply_reduce_fusion
  84.1 2.4 copy.111
  86.6 3.4 multiply_convert_fusion
  90.0 2.6 convert_reduce_fusion
  97.6 3.8 fusion.126
  101.4 3.8 fusion.99
  105.2 3.3 fusion.108
  115.8 3.7 collective-permute-start.6
  119.5 6.4 %collective-permute-start.7 = (bf16[1,4,4,3,3072]{4,1,3,2,0:T(4,128)(2,1)}, bf16[1,4,4,3,3072]{4,1,3,2,0:T(4,128)(2,1)}, u32[]{:S(2)}, u32[]{:S(2)}) collective-permute-start(bf16[1,4,4,3,3072]{4,1,3,2,0:T(4,128)(2,1)} %constant_dynamic-update-slice_fusion.2), channel_id=1, source_target_pairs={{0,2},{1,3},{2,4},{3,5},{4,6},{5,7},{6,8},{7,9},{8,10},{9,11},{10,... | collective-permute-start | bytes 884744 | tf_op jit(solution)/shard_map/ppermute | solution.py:20
  126.0 5.4 %collective-permute-start.8 = (bf16[1,4,4,3,3072]{4,1,3,2,0:T(4,128)(2,1)}, bf16[1,4,4,3,3072]{4,1,3,2,0:T(4,128)(2,1)}, u32[]{:S(2)}, u32[]{:S(2)}) collective-permute-start(bf16[1,4,4,3,3072]{4,1,3,2,0:T(4,128)(2,1)} %constant_dynamic-update-slice_fusion.2), channel_id=1, source_target_pairs={{0,3},{1,4},{2,5},{3,6},{4,7},{5,8},{6,9},{7,10},{8,11},{9,12},{10... | collective-permute-start | bytes 884744 | tf_op jit(solution)/shard_map/ppermute | solution.py:20
  131.9 2.5 multiply_reduce_fusion.1
  135.8 1.9 collective-permute-start.9
  141.9 83.9 %all-reduce = (f32[49,192]{1,0:T(8,128)}, f32[192]{0:T(256)}, f32[192]{0:T(256)}, f32[768]{0:T(1024)}, f32[192]{0:T(256)}) all-reduce(f32[49,192]{1,0:T(8,128)S(1)} %broadcast_multiply_fusion, f32[192]{0:T(256)S(1)} %broadcast_multiply_fusion.7, ...), channel_id=1, replica_groups=mesh['dp'=4,'tiles'=64] {'dp','tiles'}, use_global_device_ids=true, to_apply=%region_54.56 | all-reduce | flops 10752 | bytes 86016 | tf_op jit(solution)/shard_map/psum | solution.py:179
  225.8 11.6 %concatenate.146 = bf16[1,29,4,3,3072]{4,1,3,2,0:T(8,128)(2,1)S(1)} concatenate(bf16[1,4,4,3,3072]{4,1,3,2,0:T(4,128)(2,1)} %constant_dynamic-update-slice_fusion.2, bf16[1,4,4,3,3072]{4,1,3,2,0:T(4,128)(2,1)} %collective-permute-done.6, bf16[1,4,4,3,3072]{4,1,3,2,0:T(4,128)(2,1)} %collective-permute-done.7, bf16[1,4,4,3,3072]{4,1,3,2,0:T(4,128)(2,1)} %collective-permute-done.8, ...), dimensions={1} | concatenate | bytes 4276224 | tf_op jit(solution)/shard_map/concatenate | solution.py:65
  237.4 3.4 copy.136
  240.9 3.1 gather_fusion.1
  248.0 8.3 %multiply_convert_fusion.1 = bf16[1,4,16,16,192]{4,3,2,1,0:T(8,128)(2,1)S(1)} fusion(f32[1,4,16,16,192]{4,3,2,1,0:T(8,128)S(1)} %copy-done.2, bf16[1,4,16,16,192]{4,3,2,1,0:T(8,128)(2,1)S(1)} %bitcast.273, bf16[1,4,16,3,192]{4,3,2,1,0:T(4,128)(2,1)S(1)} %bitcast.278, bf16[1,4,16,3,192]{4,3,2,1,0:T(4,128)(2,1)S(1)} %bitcast.280, ...), kind=kLoop, calls=%fused_computation.232 | loop fusion | flops 33030144 | bytes 18277120 | tf_op jit(solution)/shard_map/convert_element_type | solution.py:177
  257.6 145.7 %all-reduce.4.cloned.1.call-done = (f32[192,768]{1,0:T(8,128)}, f32[768,192]{0,1:T(8,128)}) async-done(((f32[192,768]{1,0:T(8,128)}, f32[768,192]{0,1:T(8,128)}), (f32[192,768]{1,0:T(8,128)}, f32[768,192]{0,1:T(8,128)})) %all-reduce.4.cloned.1.call-update) | async-done | bytes 1179664 | tf_op jit(solution)/shard_map/psum | solution.py:179
  403.3 1.9 copy.181
  405.2 1.9 copy.182
  (393 shorter events, 38.6 us)
Async XLA Ops:
  7.2 79.4 %copy-start = (bf16[192,768]{1,0:T(8,128)(2,1)S(1)}, bf16[192,768]{1,0:T(8,128)(2,1)}, u32[]{:S(2)}) copy-start(bf16[192,768]{1,0:T(8,128)(2,1)} %param.21) | copy-start | bytes 884740
  7.2 396.1 %all-reduce.4.cloned.1.call-start = ((), (), s32[]{:S(2)}) async-start(), calls=%async_computation | async-start | bytes 2359296 | tf_op jit(solution)/shard_map/psum | solution.py:179
  9.7 19.0 %copy-start.133 = (s32[4,8]{1,0:T(4,128)S(1)}, s32[4,8]{1,0:T(4,128)}, u32[]{:S(2)}) copy-start(s32[4,8]{1,0:T(4,128)} %param.17) | copy-start | bytes 388
  9.7 20.7 %copy-start.3 = (bf16[1,4,16,3072]{3,2,1,0:T(8,128)(2,1)S(1)}, bf16[1,4,16,3072]{3,2,1,0:T(8,128)(2,1)}, u32[]{:S(2)}) copy-start(bf16[1,4,16,3072]{3,2,1,0:T(8,128)(2,1)} %param.15) | copy-start | bytes 1179652
  9.9 21.1 %copy-start.8 = (bf16[1,4,16,3072]{3,2,1,0:T(8,128)(2,1)S(1)}, bf16[1,4,16,3072]{3,2,1,0:T(8,128)(2,1)}, u32[]{:S(2)}) copy-start(bf16[1,4,16,3072]{3,2,1,0:T(8,128)(2,1)} %param.25) | copy-start | bytes 1179652
  13.4 24.1 %collective-permute-start = (bf16[1,4,4,3,3072]{4,1,3,2,0:T(4,128)(2,1)}, bf16[1,4,4,3,3072]{4,1,3,2,0:T(4,128)(2,1)}, u32[]{:S(2)}, u32[]{:S(2)}) collective-permute-start(bf16[1,4,4,3,3072]{4,1,3,2,0:T(4,128)(2,1)} %constant_dynamic-update-slice_fusion), channel_id=1, source_target_pairs={{0,1},{1,2},{2,3},{3,4},{4,5},{5,6},{6,7},{7,8},{8,9},{9,10},{10,1... | collective-permute-start | bytes 884744 | tf_op jit(solution)/shard_map/ppermute | solution.py:20
  18.0 22.0 %collective-permute-start.1 = (bf16[1,4,4,3,3072]{4,1,3,2,0:T(4,128)(2,1)}, bf16[1,4,4,3,3072]{4,1,3,2,0:T(4,128)(2,1)}, u32[]{:S(2)}, u32[]{:S(2)}) collective-permute-start(bf16[1,4,4,3,3072]{4,1,3,2,0:T(4,128)(2,1)} %constant_dynamic-update-slice_fusion), channel_id=1, source_target_pairs={{0,2},{1,3},{2,4},{3,5},{4,6},{5,7},{6,8},{7,9},{8,10},{9,11},{10,... | collective-permute-start | bytes 884744 | tf_op jit(solution)/shard_map/ppermute | solution.py:20
  21.9 18.1 %collective-permute-start.2 = (bf16[1,4,4,3,3072]{4,1,3,2,0:T(4,128)(2,1)}, bf16[1,4,4,3,3072]{4,1,3,2,0:T(4,128)(2,1)}, u32[]{:S(2)}, u32[]{:S(2)}) collective-permute-start(bf16[1,4,4,3,3072]{4,1,3,2,0:T(4,128)(2,1)} %constant_dynamic-update-slice_fusion), channel_id=1, source_target_pairs={{0,3},{1,4},{2,5},{3,6},{4,7},{5,8},{6,9},{7,10},{8,11},{9,12},{10... | collective-permute-start | bytes 884744 | tf_op jit(solution)/shard_map/ppermute | solution.py:20
  25.4 14.6 %collective-permute-start.3 = (bf16[1,4,4,3,3072]{4,1,3,2,0:T(4,128)(2,1)}, bf16[1,4,4,3,3072]{4,1,3,2,0:T(4,128)(2,1)}, u32[]{:S(2)}, u32[]{:S(2)}) collective-permute-start(bf16[1,4,4,3,3072]{4,1,3,2,0:T(4,128)(2,1)} %constant_dynamic-update-slice_fusion), channel_id=1, source_target_pairs={{1,0},{2,1},{3,2},{4,3},{5,4},{6,5},{7,6},{8,7},{9,8},{10,9},{11,1... | collective-permute-start | bytes 884744 | tf_op jit(solution)/shard_map/ppermute | solution.py:20
  27.3 12.6 %collective-permute-start.4 = (bf16[1,4,4,3,3072]{4,1,3,2,0:T(4,128)(2,1)}, bf16[1,4,4,3,3072]{4,1,3,2,0:T(4,128)(2,1)}, u32[]{:S(2)}, u32[]{:S(2)}) collective-permute-start(bf16[1,4,4,3,3072]{4,1,3,2,0:T(4,128)(2,1)} %constant_dynamic-update-slice_fusion), channel_id=1, source_target_pairs={{2,0},{3,1},{4,2},{5,3},{6,4},{7,5},{8,6},{9,7},{10,8},{11,9},{12,... | collective-permute-start | bytes 884744 | tf_op jit(solution)/shard_map/ppermute | solution.py:20
  29.7 40.0 %copy-start.131 = (pred[32]{0:T(512)(128)(4,1)}, pred[32]{0:T(512)(128)(4,1)S(1)}, u32[]{:S(2)}) copy-start(pred[32]{0:T(512)(128)(4,1)S(1)} %compare_and_fusion) | copy-start | bytes 100
  37.4 35.1 %copy-start.13 = (f32[1,192]{1,0:T(1,128)}, f32[1,192]{1,0:T(1,128)S(1)}, u32[]{:S(2)}) copy-start(f32[1,192]{1,0:T(1,128)S(1)} %get-tuple-element.115) | copy-start | bytes 2308
  37.4 35.1 %copy-start.15 = (f32[1,192]{1,0:T(1,128)}, f32[1,192]{1,0:T(1,128)S(1)}, u32[]{:S(2)}) copy-start(f32[1,192]{1,0:T(1,128)S(1)} %get-tuple-element.116) | copy-start | bytes 2308
  37.4 35.1 %copy-start.17 = (f32[1,192]{1,0:T(1,128)}, f32[1,192]{1,0:T(1,128)S(1)}, u32[]{:S(2)}) copy-start(f32[1,192]{1,0:T(1,128)S(1)} %get-tuple-element.117) | copy-start | bytes 2308
  37.5 35.1 %copy-start.19 = (f32[1,192]{1,0:T(1,128)}, f32[1,192]{1,0:T(1,128)S(1)}, u32[]{:S(2)}) copy-start(f32[1,192]{1,0:T(1,128)S(1)} %get-tuple-element.118) | copy-start | bytes 2308
  37.5 35.1 %copy-start.21 = (f32[1,192]{1,0:T(1,128)}, f32[1,192]{1,0:T(1,128)S(1)}, u32[]{:S(2)}) copy-start(f32[1,192]{1,0:T(1,128)S(1)} %get-tuple-element.119) | copy-start | bytes 2308
  37.5 35.1 %copy-start.23 = (f32[1,192]{1,0:T(1,128)}, f32[1,192]{1,0:T(1,128)S(1)}, u32[]{:S(2)}) copy-start(f32[1,192]{1,0:T(1,128)S(1)} %get-tuple-element.120) | copy-start | bytes 2308
  37.5 10.9 %collective-permute-start.5 = (bf16[1,4,4,3,3072]{4,1,3,2,0:T(4,128)(2,1)}, bf16[1,4,4,3,3072]{4,1,3,2,0:T(4,128)(2,1)S(1)}, u32[]{:S(2)}, u32[]{:S(2)}) collective-permute-start(bf16[1,4,4,3,3072]{4,1,3,2,0:T(4,128)(2,1)} %constant_dynamic-update-slice_fusion), channel_id=1, source_target_pairs={{3,0},{4,1},{5,2},{6,3},{7,4},{8,5},{9,6},{10,7},{11,8},{12,9},{13... | collective-permute-start | bytes 884744 | tf_op jit(solution)/shard_map/ppermute | solution.py:20
  39.3 27.4 %copy-start.89 = (s32[1024]{0:T(1024)}, s32[1024]{0:T(1024)S(1)}, u32[]{:S(2)}) copy-start(s32[1024]{0:T(1024)S(1)} %pad_clamp_fusion) | copy-start | bytes 12292
  109.9 21.9 %copy-start.139 = (f32[192]{0:T(256)S(1)}, f32[192]{0:T(256)}, u32[]{:S(2)}) copy-start(f32[192]{0:T(256)} %get-tuple-element.64) | copy-start | bytes 2308
  109.9 21.9 %copy-start.138 = (f32[192]{0:T(256)S(1)}, f32[192]{0:T(256)}, u32[]{:S(2)}) copy-start(f32[192]{0:T(256)} %get-tuple-element.10) | copy-start | bytes 2308
  109.9 21.9 %copy-start.103 = (f32[768]{0:T(1024)S(1)}, f32[768]{0:T(1024)}, u32[]{:S(2)}) copy-start(f32[768]{0:T(1024)} %get-tuple-element.167) | copy-start | bytes 9220
  109.9 21.9 %copy-start.6 = (f32[1024,192]{0,1:T(8,128)S(1)}, f32[1024,192]{0,1:T(8,128)}, u32[]{:S(2)}) copy-start(f32[1024,192]{0,1:T(8,128)} %copy.113) | copy-start | bytes 2359300
  109.9 21.9 %copy-start.136 = (f32[192]{0:T(256)S(1)}, f32[192]{0:T(256)}, u32[]{:S(2)}) copy-start(f32[192]{0:T(256)} %param.24) | copy-start | bytes 2308
  109.9 21.9 %copy-start.137 = (pred[1024]{0:T(1024)(128)(4,1)S(1)}, pred[1024]{0:T(1024)(128)(4,1)}, u32[]{:S(2)}) copy-start(pred[1024]{0:T(1024)(128)(4,1)} %broadcast_in_dim.53) | copy-start | bytes 3076
  113.2 22.5 %collective-permute-start.10 = (bf16[1,4,4,3,3072]{4,1,3,2,0:T(4,128)(2,1)}, bf16[1,4,4,3,3072]{4,1,3,2,0:T(4,128)(2,1)}, u32[]{:S(2)}, u32[]{:S(2)}) collective-permute-start(bf16[1,4,4,3,3072]{4,1,3,2,0:T(4,128)(2,1)} %constant_dynamic-update-slice_fusion.2), channel_id=1, source_target_pairs={{2,0},{3,1},{4,2},{5,3},{6,4},{7,5},{8,6},{9,7},{10,8},{11,9},{12,... | collective-permute-start | bytes 884744 | tf_op jit(solution)/shard_map/ppermute | solution.py:20
  114.5 111.2 %collective-permute-start.11 = (bf16[1,4,4,3,3072]{4,1,3,2,0:T(4,128)(2,1)}, bf16[1,4,4,3,3072]{4,1,3,2,0:T(4,128)(2,1)}, u32[]{:S(2)}, u32[]{:S(2)}) collective-permute-start(bf16[1,4,4,3,3072]{4,1,3,2,0:T(4,128)(2,1)} %constant_dynamic-update-slice_fusion.2), channel_id=1, source_target_pairs={{3,0},{4,1},{5,2},{6,3},{7,4},{8,5},{9,6},{10,7},{11,8},{12,9},{13... | collective-permute-start | bytes 884744 | tf_op jit(solution)/shard_map/ppermute | solution.py:20
  115.8 109.9 %collective-permute-start.6 = (bf16[1,4,4,3,3072]{4,1,3,2,0:T(4,128)(2,1)}, bf16[1,4,4,3,3072]{4,1,3,2,0:T(4,128)(2,1)}, u32[]{:S(2)}, u32[]{:S(2)}) collective-permute-start(bf16[1,4,4,3,3072]{4,1,3,2,0:T(4,128)(2,1)} %constant_dynamic-update-slice_fusion.2), channel_id=1, source_target_pairs={{0,1},{1,2},{2,3},{3,4},{4,5},{5,6},{6,7},{7,8},{8,9},{9,10},{10,1... | collective-permute-start | bytes 884744 | tf_op jit(solution)/shard_map/ppermute | solution.py:20
  119.5 106.2 %collective-permute-start.7 = (bf16[1,4,4,3,3072]{4,1,3,2,0:T(4,128)(2,1)}, bf16[1,4,4,3,3072]{4,1,3,2,0:T(4,128)(2,1)}, u32[]{:S(2)}, u32[]{:S(2)}) collective-permute-start(bf16[1,4,4,3,3072]{4,1,3,2,0:T(4,128)(2,1)} %constant_dynamic-update-slice_fusion.2), channel_id=1, source_target_pairs={{0,2},{1,3},{2,4},{3,5},{4,6},{5,7},{6,8},{7,9},{8,10},{9,11},{10,... | collective-permute-start | bytes 884744 | tf_op jit(solution)/shard_map/ppermute | solution.py:20
  126.0 99.8 %collective-permute-start.8 = (bf16[1,4,4,3,3072]{4,1,3,2,0:T(4,128)(2,1)}, bf16[1,4,4,3,3072]{4,1,3,2,0:T(4,128)(2,1)}, u32[]{:S(2)}, u32[]{:S(2)}) collective-permute-start(bf16[1,4,4,3,3072]{4,1,3,2,0:T(4,128)(2,1)} %constant_dynamic-update-slice_fusion.2), channel_id=1, source_target_pairs={{0,3},{1,4},{2,5},{3,6},{4,7},{5,8},{6,9},{7,10},{8,11},{9,12},{10... | collective-permute-start | bytes 884744 | tf_op jit(solution)/shard_map/ppermute | solution.py:20
  135.8 90.0 %collective-permute-start.9 = (bf16[1,4,4,3,3072]{4,1,3,2,0:T(4,128)(2,1)}, bf16[1,4,4,3,3072]{4,1,3,2,0:T(4,128)(2,1)}, u32[]{:S(2)}, u32[]{:S(2)}) collective-permute-start(bf16[1,4,4,3,3072]{4,1,3,2,0:T(4,128)(2,1)} %constant_dynamic-update-slice_fusion.2), channel_id=1, source_target_pairs={{1,0},{2,1},{3,2},{4,3},{5,4},{6,5},{7,6},{8,7},{9,8},{10,9},{11,1... | collective-permute-start | bytes 884744 | tf_op jit(solution)/shard_map/ppermute | solution.py:20
  138.3 87.5 %copy-start.10 = (bf16[1,1,4,3,3072]{4,1,3,2,0:T(2,128)(2,1)S(1)}, bf16[1,1,4,3,3072]{4,1,3,2,0:T(2,128)(2,1)}, u32[]{:S(2)}) copy-start(bf16[1,1,4,3,3072]{4,1,3,2,0:T(2,128)(2,1)} %copy-done.9) | copy-start | bytes 221188
  (124 other events, 264.2 us)
Sparse Core Ops, SparseCore 0:
  140.0 263.2 all-reduce.3
where the time goes:
time: 422 us; the launch traced here: 414 us
  waiting for transfers between devices  154 us (36%)
  blocking collectives  83.9 us (20%)
  local copies, waits for them, and re-layouts  74.2 us (18%)
  starting transfers between devices  37.1 us (9%)
  other arithmetic  35.4 us (8%)
  between operations  16.9 us (4%)
  matrix products  12.6 us (3%)
    psum x1, waiting for transfers between devices, shards(): lax.psum((grad_kernel_part, grad_gain_part, grad_shift_part, grad_in_part...  146 us
    psum x1, blocking collectives, shards(): lax.psum((grad_kernel_part, grad_gain_part, grad_shift_part, grad_in_part...  83.9 us
    ppermute x12, starting transfers between devices, shifted_2(): return lax.ppermute(block, axis, route)  37 us
    concatenate x2, local copies, waits for them, and re-layouts, extend_tiles(): jnp.concatenate([borders] + from_below + from_above + [jnp.zeros_like(bor...  24.7 us
    reduce_sum x5, other arithmetic, kernel_grad(): jnp.sum(window.astype(jnp.float32) * back_values, axis=axes_all)  11.2 us
    reduce_sum x1, other arithmetic, shards(): mean_val = jnp.mean(conv_rows, axis=-1, keepdims=True)  9.38 us
    unnamed x302, local copies, waits for them, and re-layouts  8.71 us
    reshape x2, local copies, waits for them, and re-layouts, extend_tiles(): flat_rims = stacked.reshape(samples, -1, 3, width)  8.55 us
  transfers between devices with their start and end apart: 13, of which 2 were waited for; matrix products, arithmetic and copies ran while one was open for 12% of the time, Pallas kernels for 0%

commit v1 on v0

v1 whole, which is shorter than its diff:
```python
import functools
import math

import jax
import jax.numpy as jnp
from jax import lax
from jax.experimental import pallas as pl
from jax.experimental.pallas import tpu as pltpu
from jax.sharding import PartitionSpec as P

KS = 7
TAPS = KS * KS
TPD = 4
TILE = 16
C = 192
HID = 768
WIDTH = TILE * C
BLOCKS = WIDTH // 128
PAD_BLOCKS = 36
STRIP = 80
CELLS = TILE * TILE
INV_SQRT2 = 0.7071067811865476
INV_SQRT_2PI = 0.3989422804014327
EXTRA = 128
HALF_ROWS = 6 * C + EXTRA // 2
F32 = jnp.float32
BF16 = jnp.bfloat16
VMEM_LIMIT = 20 * 1024 * 1024


def low_lanes(rows):
    return lax.broadcasted_iota(jnp.int32, (rows, 128), 1) < 64


def expand_mask(mask_ref, s):
    cell = lax.broadcasted_iota(jnp.int32, (TILE, WIDTH), 0) * C
    lane = lax.broadcasted_iota(jnp.int32, (TILE, WIDTH), 1)
    spread = jnp.where((lane >= cell) & (lane < cell + C), 1.0, 0.0).astype(BF16)
    keep = (mask_ref[s] > 0).astype(F32).astype(BF16)
    return jnp.dot(keep, spread, preferred_element_type=F32)


def chip_is_even():
    return lax.rem(lax.div(lax.axis_index("tiles"), 2), 2) == 0


def core_is_first():
    return lax.rem(lax.axis_index("tiles"), 2) == 0


def emit_strips(tile_block, strip, early, late, far, right_own, left_own):
    even, first_core = chip_is_even(), core_is_first()
    higher, lower = jnp.where(even, 0, 1), jnp.where(even, 1, 0)

    def put(place, entry, rows, values):
        @pl.when(place == 0)
        def _():
            early[entry, rows, :] = values

        @pl.when(place == 1)
        def _():
            late[entry, rows, :] = values

    everything = slice(0, STRIP)
    strip[72:80, :] = jnp.zeros((8, 128), F32)
    for s in range(TPD):
        for t in range(BLOCKS):
            strip[3 * t : 3 * t + 3, :] = tile_block(s, t, 13, 3)
        top = strip[...].astype(BF16)
        put(higher, s, everything, top)
        for t in range(BLOCKS):
            strip[3 * t : 3 * t + 3, :] = tile_block(s, t, 0, 3)
        bottom = strip[...].astype(BF16)
        put(lower, s, everything, bottom)
        if s == 0:

            @pl.when(first_core)
            def _(bottom=bottom):
                far[0] = bottom

        if s == TPD - 1:

            @pl.when(jnp.logical_not(first_core))
            def _(top=top):
                far[0] = top

        for t in range(5):
            rows = slice(16 * t, 16 * t + 16)
            right = tile_block(s, 19 + t, 0, 16).astype(BF16)
            left = tile_block(s, t, 0, 16).astype(BF16)
            if s == TPD - 1:
                put(higher, TPD, rows, right)
            else:
                right_own[s, rows, :] = right
            if s == 0:
                put(lower, TPD, rows, left)
            else:
                left_own[s - 1, rows, :] = left


def strip_shapes():
    return [jax.ShapeDtypeStruct((n, STRIP, 128), BF16) for n in (TPD + 1, TPD + 1, 1, TPD - 1, TPD - 1)]


def by_chip(early, late, came_early, came_late, work):
    even = chip_is_even()

    @pl.when(even)
    def _():
        work(early, late, came_late, came_early)

    @pl.when(jnp.logical_not(even))
    def _():
        work(late, early, came_early, came_late)


def by_core(first, second):
    is_first = core_is_first()

    @pl.when(is_first)
    def _():
        first()

    @pl.when(jnp.logical_not(is_first))
    def _():
        second()


def relay_kernel(early, late, came_early, came_late, relay):
    def work(own_down, own_up, lower, higher):
        def fill(own, whole, one):
            for n in range(TPD + 1):
                relay[n] = own[n]
                relay[TPD + 1 + n] = whole[n]
            relay[2 * TPD + 2] = one[...]

        by_core(
            lambda: fill(own_down, higher, lower.at[TPD - 1]),
            lambda: fill(own_up, lower, higher.at[0]),
        )

    by_chip(early, late, came_early, came_late, work)


def gather_strips(given, rows_below, rows_above, right_cols, left_cols):
    early, late, right_own, left_own, came_early, came_late, came_far, relay = given
    for s in range(TPD - 1):
        right_cols[1 + s] = right_own[s]
        left_cols[1 + s] = left_own[s]

    def work(own_down, own_up, lower, higher):
        for s in range(TPD):
            rows_below[4 + s] = lower[s]
            rows_below[12 + s] = own_down[s]
            rows_above[s] = own_up[s]
            rows_above[8 + s] = higher[s]
        right_cols[TPD] = own_down[TPD]
        left_cols[0] = own_up[TPD]

    by_chip(early, late, came_early, came_late, work)

    def place(below, above, one_below, one_above):
        rows_below[3] = one_below[...]
        rows_above[12] = one_above[...]
        for s in range(TPD):
            rows_below[8 + s] = relay[below + s]
            rows_above[4 + s] = relay[above + s]
        right_cols[0] = relay[below + TPD]
        left_cols[TPD] = relay[above + TPD]

    last = 2 * TPD + 2
    by_core(
        lambda: place(TPD + 1, 0, came_far.at[0], relay.at[last]),
        lambda: place(0, TPD + 1, relay.at[last], came_far.at[0]),
    )


def fill_halo(padded, shifted, near_ref, strip, edges, tiles):
    rows_below, rows_above, right_cols, left_cols = edges
    first = lax.axis_index("tiles") * TPD

    def one_tile(s, carry):
        tile = tiles[0] + s

        def fetch(direction, source, base, count):
            slot = near_ref[tile, direction]
            place = jnp.clip(slot - first + base, 0, count - 1)
            values = source[place].astype(F32)
            return jnp.where(slot >= 0, values, 0.0)

        def put_rows(values, row, source_block, target_block, count):
            strip[...] = values
            for t in range(count):
                at = 3 * (source_block + t)
                padded[s, target_block + t, row : row + 3, :] = strip[at : at + 3, :]

        put_rows(fetch(1, rows_below, 12, 16), 5, 0, 6, BLOCKS)
        put_rows(fetch(0, rows_below, 12, 16), 5, 19, 1, 5)
        put_rows(fetch(2, rows_below, 12, 16), 5, 0, 30, 5)
        put_rows(fetch(6, rows_above, 0, 16), 24, 0, 6, BLOCKS)
        put_rows(fetch(5, rows_above, 0, 16), 24, 19, 1, 5)
        put_rows(fetch(7, rows_above, 0, 16), 24, 0, 30, 5)
        west = fetch(3, right_cols, 1, TPD + 1)
        east = fetch(4, left_cols, 0, TPD + 1)
        for t in range(5):
            padded[s, 1 + t, 8:24, :] = west[16 * t : 16 * t + 16, :]
            padded[s, 30 + t, 8:24, :] = east[16 * t : 16 * t + 16, :]
        low = low_lanes(32)
        turned = pltpu.roll(padded[s, 1], 64, 1)
        for t in range(1, 34):
            following = pltpu.roll(padded[s, t + 1], 64, 1)
            shifted[s, t] = jnp.where(low, turned, following)
            turned = following
        return carry

    lax.fori_loop(0, len(tiles), one_tile, 0)


def spread_taps(dw_ref, wide, taps):
    low = low_lanes(TAPS)
    first = dw_ref[:, 0:128]
    last = dw_ref[:, 64:192]
    wide[0, 0:TAPS, :] = first
    turned_first = pltpu.roll(first, 64, 1)
    turned_last = pltpu.roll(last, 64, 1)
    wide[1, 0:TAPS, :] = jnp.where(low, turned_last, turned_first)
    wide[2, 0:TAPS, :] = last
    for k in range(TAPS):
        for m in range(3):
            taps[3 * k + m] = jnp.broadcast_to(wide[m, k : k + 1, :], (8, 128))


def windows(padded, shifted, s, m, row):
    half = BLOCKS // 3
    even = [shifted[s, 1 + m + 3 * n, pl.ds(row, 8), :] for n in range(half + 3)]
    odd = [padded[s, 3 + m + 3 * n, pl.ds(row, 8), :] for n in range(half + 2)]
    return lambda q, j: (odd if j % 2 else even)[q + j // 2]


def depthwise(padded, shifted, taps, out, flip, count=TPD):
    half = BLOCKS // 3
    for m in range(3):

        def body(s, carry, m=m):
            for h in range(2):
                total = [None] * half
                for i in range(KS):
                    window = windows(padded, shifted, s, m, 5 + i + 8 * h)
                    for j in range(KS):
                        k = KS * i + j
                        weight = taps[3 * (TAPS - 1 - k if flip else k) + m]
                        for q in range(half):
                            term = window(q, j) * weight
                            total[q] = term if total[q] is None else total[q] + term
                for q in range(half):
                    out[s, 3 * q + m, 8 * h : 8 * h + 8, :] = total[q]
            return carry

        lax.fori_loop(0, count, body, 0)


def kernel_grad(padded, shifted, back, wide):
    half = BLOCKS // 3
    for m in range(3):
        for i in range(KS):

            def body(s, totals, m=m, i=i):
                totals = list(totals)
                for h in range(2):
                    window = windows(padded, shifted, s, m, 5 + i + 8 * h)
                    here = [back[s, 3 * q + m, 8 * h : 8 * h + 8, :] for q in range(half)]
                    for j in range(KS):
                        for q in range(half):
                            totals[j] = totals[j] + window(q, j) * here[q]
                return tuple(totals)

            start = tuple(jnp.zeros((8, 128), F32) for _ in range(KS))
            totals = lax.fori_loop(0, TPD, body, start)
            for j in range(KS):
                k = KS * i + j
                wide[m, k : k + 1, :] = jnp.sum(totals[j], axis=0, keepdims=True)


def to_rows(block, rows_ref):
    low = low_lanes(TILE)
    for q in range(TILE // 2):
        first, middle, last = block(3 * q), block(3 * q + 1), block(3 * q + 2)
        even = slice(32 * q, 32 * q + 16)
        odd = slice(32 * q + 16, 32 * q + 32)
        rows_ref[even, 0:128] = first
        rows_ref[even, 128:256] = middle
        turned = pltpu.roll(last, 64, 1)
        rows_ref[odd, 0:128] = jnp.where(low, pltpu.roll(middle, 64, 1), turned)
        rows_ref[odd, 128:256] = turned


def from_rows(rows_ref, put):
    low = low_lanes(TILE)
    for q in range(TILE // 2):
        even = slice(32 * q, 32 * q + 16)
        odd = slice(32 * q + 16, 32 * q + 32)
        turned = pltpu.roll(rows_ref[odd, 0:128], 64, 1)
        put(3 * q, rows_ref[even, 0:128])
        put(3 * q + 1, jnp.where(low, rows_ref[even, 128:256], turned))
        put(3 * q + 2, jnp.where(low, turned, pltpu.roll(rows_ref[odd, 128:256], 64, 1)))


def dot_last(left, right):
    return lax.dot_general(left, right, (((1,), (1,)), ((), ())), preferred_element_type=F32)


def dot_first(left, right):
    return lax.dot_general(left, right, (((0,), (0,)), ((), ())), preferred_element_type=F32)


def prepare_kernel(fields_far, mask_far, *refs):
    strips, (blocks, strip, fields, mask, sems) = refs[0:5], refs[5:]
    copies = [
        pltpu.make_async_copy(fields_far, fields, sems.at[0]),
        pltpu.make_async_copy(mask_far, mask, sems.at[1]),
    ]
    for copy in copies:
        copy.start()
    for copy in copies:
        copy.wait()
    for s in range(TPD):
        keep = expand_mask(mask, s) > 0.5
        values = jnp.where(keep, fields[s].astype(F32), 0.0)
        for t in range(BLOCKS):
            blocks[s, t] = values[:, 128 * t : 128 * t + 128]
    emit_strips(lambda s, t, row, rows: blocks[s, t, row : row + rows, :], strip, *strips)


def block_kernel(*refs):
    fields, cotangent, mask, near, dw, gain_ref, bias_ref, w_in_far, b_in, w_out_far, scale_ref = refs[0:11]
    given = refs[11:19]
    block_out, back_out, keep_rows, send_rows = refs[19:23]
    strips = refs[23:28]
    (
        padded, shifted_pad, keep_blocks, blocks, strip, rows_below, rows_above, right_cols, left_cols,
        wide, taps, rows_a, rows_b, norm_rows, hid_rows, bb_rows, pre_rows, sums, bias_sums, extra,
        w_in, w_out, weight_sems,
    ) = refs[28:]

    arrive_in = pltpu.make_async_copy(w_in_far, w_in, weight_sems.at[0])
    arrive_out = pltpu.make_async_copy(w_out_far, w_out, weight_sems.at[1])
    arrive_in.start()
    arrive_out.start()
    for s in range(TPD):
        keep = expand_mask(mask, s)
        values = jnp.where(keep > 0.5, fields[s].astype(F32), 0.0)
        for t in range(BLOCKS):
            padded[s, 6 + t, 8:24, :] = values[:, 128 * t : 128 * t + 128]
            keep_blocks[s, t] = keep[:, 128 * t : 128 * t + 128]
    spread_taps(dw, wide, taps)
    gather_strips(given, rows_below, rows_above, right_cols, left_cols)
    edges = (rows_below, rows_above, right_cols, left_cols)
    fill_halo(padded, shifted_pad, near, strip, edges, range(TPD))
    depthwise(padded, shifted_pad, taps, blocks, False)
    arrive_in.wait()
    arrive_out.wait()

    sums[...] = jnp.zeros_like(sums)
    bias_sums[...] = jnp.zeros_like(bias_sums)

    def one_tile(s, carry):
        gain, scale = gain_ref[...], scale_ref[...]
        to_rows(lambda t: blocks[s, t], rows_a)
        to_rows(
            lambda t: cotangent[s, :, 128 * t : 128 * t + 128].astype(F32) * keep_blocks[s, t], rows_b
        )
        conv = rows_a[:, 0:C]
        seed = rows_b[:, 0:C]
        centred = conv - jnp.mean(conv, axis=-1, keepdims=True)
        inv_std = lax.rsqrt(jnp.mean(centred * centred, axis=-1, keepdims=True) + 1e-06)
        normed = centred * inv_std
        shifted = (normed * gain + bias_ref[...]).astype(BF16)
        norm_rows[s] = shifted
        preact = jnp.dot(shifted, w_in[...], preferred_element_type=F32) + b_in[...]
        bell = jnp.exp(-0.5 * preact * preact)
        u = 1.0 / (1.0 + (0.3275911 * INV_SQRT2) * jnp.abs(preact))
        series = u * (
            0.5 * 0.254829592
            + u * (0.5 * -0.284496736 + u * (0.5 * 1.421413741 + u * (0.5 * -1.453152027 + u * (0.5 * 1.061405429))))
        )
        tail = series * bell
        cdf = jnp.where(preact >= 0.0, 1.0 - tail, tail)
        hidden = (preact * cdf).astype(BF16)
        hid_rows[s] = hidden
        slope = cdf + preact * bell * INV_SQRT_2PI
        branch = dot_last(hidden, w_out[...])
        rows_a[:, 0:C] = branch * scale

        def put_out(t, values):
            total = padded[s, 6 + t, 8:24, :] + values
            block_out[s, :, 128 * t : 128 * t + 128] = (keep_blocks[s, t] * total).astype(BF16)

        from_rows(rows_a, put_out)
        sums[0:1, 0:C] += jnp.sum(seed * branch, axis=0, keepdims=True)
        back_branch = (seed * scale).astype(BF16)
        bb_rows[s] = back_branch
        back_pre = (jnp.dot(back_branch, w_out[...], preferred_element_type=F32) * slope).astype(BF16)
        pre_rows[s] = back_pre
        bias_sums[...] += jnp.sum(back_pre.astype(F32), axis=0, keepdims=True)
        back_shift = dot_last(back_pre, w_in[...])
        sums[1:2, 0:C] += jnp.sum(back_shift * normed, axis=0, keepdims=True)
        sums[2:3, 0:C] += jnp.sum(back_shift, axis=0, keepdims=True)
        scaled = back_shift * gain
        back = inv_std * (
            scaled
            - jnp.mean(scaled, axis=-1, keepdims=True)
            - normed * jnp.mean(scaled * normed, axis=-1, keepdims=True)
        )
        rows_b[:, 0:C] = back.astype(BF16).astype(F32)

        def put_back(t, values):
            blocks[s, t] = values
            back_out[s, :, 128 * t : 128 * t + 128] = values.astype(BF16)

        from_rows(rows_b, put_back)
        return carry

    lax.fori_loop(0, TPD, one_tile, 0)

    emit_strips(lambda s, t, row, rows: blocks[s, t, row : row + rows, :], strip, *strips)
    kernel_grad(padded, shifted_pad, blocks, wide)
    low = low_lanes(TAPS)
    first, middle, last = wide[0, 0:TAPS, :], wide[1, 0:TAPS, :], wide[2, 0:TAPS, :]
    turned_middle, turned_last = pltpu.roll(middle, 64, 1), pltpu.roll(last, 64, 1)
    extra[...] = jnp.zeros_like(extra)
    extra[0:TAPS, :] = first + jnp.where(low, turned_middle, turned_last)
    extra[56 : 56 + TAPS, :] = jnp.where(low, middle + turned_last, 0.0)
    for n in range(3):
        extra[112 + 2 * n : 113 + 2 * n, :] = sums[n : n + 1, 0:128]
        extra[113 + 2 * n : 114 + 2 * n, :] = sums[n : n + 1, 128:256]
    for n in range(6):
        extra[118 + n : 119 + n, :] = bias_sums[0:1, 128 * n : 128 * n + 128]
    grad_in = dot_first(norm_rows[...].reshape(TPD * CELLS, C), pre_rows[...].reshape(TPD * CELLS, HID))
    grad_out = dot_first(bb_rows[...].reshape(TPD * CELLS, C), hid_rows[...].reshape(TPD * CELLS, HID))
    core = lax.rem(lax.axis_index("tiles"), 2)

    def write(target, grad, part, kind):
        for n in range(6):
            target[C * n : C * n + C, :] = grad[:, 128 * n : 128 * n + 128].astype(kind)
        target[6 * C : HALF_ROWS, :] = extra[part * (EXTRA // 2) : (part + 1) * (EXTRA // 2), :].astype(kind)

    @pl.when(core == 0)
    def _():
        write(keep_rows, grad_in, 0, F32)
        write(send_rows, grad_out, 1, BF16)

    @pl.when(core == 1)
    def _():
        write(keep_rows, grad_out, 1, F32)
        write(send_rows, grad_in, 0, BF16)


def field_grad_kernel(tile, *refs):
    back, cotangent, mask, near, dw = refs[0:5]
    given, out = refs[5:13], refs[13]
    padded, shifted_pad, blocks, strip, rows_below, rows_above, right_cols, left_cols, wide, taps = refs[14:]
    for t in range(BLOCKS):
        padded[0, 6 + t, 8:24, :] = back[tile, :, 128 * t : 128 * t + 128].astype(F32)
    spread_taps(dw, wide, taps)
    gather_strips(given, rows_below, rows_above, right_cols, left_cols)
    edges = (rows_below, rows_above, right_cols, left_cols)
    fill_halo(padded, shifted_pad, near, strip, edges, range(tile, tile + 1))
    depthwise(padded, shifted_pad, taps, blocks, True, 1)
    keep = expand_mask(mask, tile)
    for t in range(BLOCKS):
        lanes = slice(128 * t, 128 * t + 128)
        total = cotangent[tile, :, lanes].astype(F32) + blocks[0, t]
        out[0, :, lanes] = (keep[:, lanes] * total).astype(BF16)


def unpack_kernel(rows, grad_kernel, gain, shift, grad_in, bias, grad_out, scale):
    factor = 1.0 / math.sqrt(4 * 64 * TPD * CELLS)

    for n in range(6):
        grad_in[:, 128 * n : 128 * n + 128] = rows[C * n : C * n + C, :].astype(F32) * factor
        at = HALF_ROWS + C * n
        grad_out[:, 128 * n : 128 * n + 128] = rows[at : at + C, :].astype(F32) * factor
    first_part = rows[6 * C : HALF_ROWS, :].astype(F32) * factor
    last_part = rows[HALF_ROWS + 6 * C :, :].astype(F32) * factor
    grad_kernel[:, 0:128] = first_part[0:TAPS, :]
    both = jnp.concatenate([first_part[56:64, :], last_part[0:48, :]], axis=0)
    grad_kernel[:, 128:192] = both[0:TAPS, 0:64]
    tail = last_part[48:64, :]
    for n, target in ((0, scale), (1, gain), (2, shift)):
        target[:, 0:128] = tail[2 * n : 2 * n + 1, :]
        target[:, 128:192] = tail[2 * n + 1 : 2 * n + 2, 0:64]
    for n in range(6):
        bias[128 * n : 128 * n + 128] = tail[6 + n, :]


def whole(memory=pltpu.VMEM):
    return pl.BlockSpec(memory_space=memory)


def call(kernel, inputs, out_shape, scratch, cost, smem=(), far=()):
    place = lambda n: pltpu.SMEM if n in smem else pl.ANY if n in far else pltpu.VMEM
    return pl.pallas_call(
        kernel,
        out_shape=out_shape,
        in_specs=[whole(place(n)) for n in range(len(inputs))],
        out_specs=jax.tree.map(lambda _: whole(), out_shape),
        scratch_shapes=scratch,
        compiler_params=pltpu.CompilerParams(vmem_limit_bytes=VMEM_LIMIT),
        cost_estimate=pl.CostEstimate(flops=cost, bytes_accessed=4000000, transcendentals=0),
    )(*inputs)


def halo_scratch():
    return [
        pltpu.VMEM((STRIP, 128), F32),
        pltpu.VMEM((16, STRIP, 128), BF16),
        pltpu.VMEM((16, STRIP, 128), BF16),
        pltpu.VMEM((TPD + 1, STRIP, 128), BF16),
        pltpu.VMEM((TPD + 1, STRIP, 128), BF16),
    ]


def swap(block, axis, partner):
    count = lax.axis_size(axis)
    return lax.ppermute(block, axis, [(i, partner(i)) for i in range(count) if 0 <= partner(i) < count])


def chip_up(i):
    return i ^ 2


def chip_down(i):
    return ((i // 2 + 1) ^ 1) * 2 - 2 + i % 2


def three_away(i):
    return i + 3 if i % 2 else i - 3


def other_core(i):
    return i ^ 1


def relay(early, late, came_early, came_late):
    shape = jax.ShapeDtypeStruct((2 * TPD + 3, STRIP, 128), BF16)
    return call(relay_kernel, (early, late, came_early, came_late), shape, [], 10**5)


def exchange_strips(strips):
    early, late, far, right_own, left_own = strips
    came_early = swap(early, "tiles", chip_up)
    came_late = swap(late, "tiles", chip_down)
    came_far = swap(far, "tiles", three_away)
    passed = swap(relay(early, late, came_early, came_late), "tiles", other_core)
    return (early, late, right_own, left_own, came_early, came_late, came_far, passed)


def reduce_and_exchange(keep, send, strips, finish):
    early, late, far, right_own, left_own = strips
    place = lax.axis_index("tiles")
    core, y = place % 2, (place // 2) % 4
    x = lax.axis_index("dp")

    def halves(block, bit):
        n = block.shape[0] // 2
        own = lax.dynamic_slice_in_dim(block, bit * n, n, 0)
        return own, lax.dynamic_slice_in_dim(block, (1 - bit) * n, n, 0).astype(BF16)

    def join(block, axis, partner, bit):
        other = swap(block, axis, partner)
        return jnp.where(bit == 0, jnp.concatenate([block, other], 0), jnp.concatenate([other, block], 0))

    first_x, second_x, first_y = (x + x // 2) % 2, x // 2, (y + y // 2) % 2
    came, came_early = lax.optimization_barrier((swap(send, "tiles", other_core), swap(early, "tiles", chip_up)))
    own, other = halves(keep + came.astype(F32), first_x)
    came, came_late = lax.optimization_barrier((swap(other, "dp", lambda i: i ^ 1), swap(late, "tiles", chip_down)))
    own, other = halves(own + came.astype(F32), second_x)
    between = relay(early, late, came_early, came_late)
    came, passed = lax.optimization_barrier((swap(other, "dp", lambda i: i ^ 3), swap(between, "tiles", other_core)))
    own, other = halves(own + came.astype(F32), first_y)
    came, came_far = lax.optimization_barrier((swap(other, "tiles", lambda i: i ^ 2), swap(far, "tiles", three_away)))
    mine = own + came.astype(F32)
    given = (early, late, right_own, left_own, came_early, came_late, came_far, passed)
    parts = []
    for tile, mask in enumerate((6, 8, 24, 56)):
        sent, given = lax.optimization_barrier((mine.astype(BF16), given))
        came, part = lax.optimization_barrier((swap(sent, "tiles", lambda i: i ^ mask), finish(tile, given)))
        parts.append(part)
        mine = sent.astype(F32) + came.astype(F32)
    mine = mine.astype(BF16)
    mine = join(mine, "tiles", lambda i: i ^ 2, first_y)
    mine = join(mine, "dp", lambda i: i ^ 3, second_x)
    mine = join(mine, "dp", lambda i: i ^ 1, first_x)
    return join(mine, "tiles", other_core, core), jnp.concatenate(parts, 0)


def shards(
    fields, ocean_mask, neighbours, dw_kernel, ln_gain, ln_bias, w_in, b_in, w_out, layer_scale, cotangent
):
    tiles = fields.reshape(TPD, TILE, WIDTH)
    cot = cotangent.reshape(TPD, TILE, WIDTH)
    tile_shape = jax.ShapeDtypeStruct((TPD, TILE, WIDTH), BF16)
    block_scratch = pltpu.VMEM((TPD, BLOCKS, TILE, 128), F32)
    pad_scratch = pltpu.VMEM((TPD, PAD_BLOCKS, 32, 128), F32)
    tap_scratch = [pltpu.VMEM((3, 56, 128), F32), pltpu.VMEM((3 * TAPS, 8, 128), F32)]

    strips = call(
        prepare_kernel,
        (tiles, ocean_mask),
        strip_shapes(),
        [
            block_scratch,
            pltpu.VMEM((STRIP, 128), F32),
            pltpu.VMEM((TPD, TILE, WIDTH), BF16),
            pltpu.VMEM((TPD, TILE, TILE), jnp.int32),
            pltpu.SemaphoreType.DMA((2,)),
        ],
        10**6,
        far=(0, 1),
    )
    given = exchange_strips(strips)
    row = lambda v: v.reshape(1, -1)
    outs = call(
        block_kernel,
        (
            tiles, cot, ocean_mask, neighbours, dw_kernel, row(ln_gain), row(ln_bias), w_in, row(b_in), w_out.T,
            row(layer_scale), *given,
        ),
        [
            tile_shape,
            tile_shape,
            jax.ShapeDtypeStruct((HALF_ROWS, 128), F32),
            jax.ShapeDtypeStruct((HALF_ROWS, 128), BF16),
            *strip_shapes(),
        ],
        [
            pad_scratch, pad_scratch, block_scratch, block_scratch, *halo_scratch(), *tap_scratch,
            pltpu.VMEM((CELLS, 256), F32),
            pltpu.VMEM((CELLS, 256), F32),
            pltpu.VMEM((TPD, CELLS, C), BF16),
            pltpu.VMEM((TPD, CELLS, HID), BF16),
            pltpu.VMEM((TPD, CELLS, C), BF16),
            pltpu.VMEM((TPD, CELLS, HID), BF16),
            pltpu.VMEM((8, 256), F32),
            pltpu.VMEM((1, HID), F32),
            pltpu.VMEM((EXTRA, 128), F32),
            pltpu.VMEM((C, HID), BF16),
            pltpu.VMEM((C, HID), BF16),
            pltpu.SemaphoreType.DMA((2,)),
        ],
        2 * 10**9,
        smem=(3,),
        far=(7, 9),
    )
    block_out, back, keep_rows, send_rows = outs[0:4]

    def finish(tile, given):
        return call(
            functools.partial(field_grad_kernel, tile),
            (back, cot, ocean_mask, neighbours, dw_kernel, *given),
            jax.ShapeDtypeStruct((1, TILE, WIDTH), BF16),
            [
                pltpu.VMEM((1, PAD_BLOCKS, 32, 128), F32),
                pltpu.VMEM((1, PAD_BLOCKS, 32, 128), F32),
                pltpu.VMEM((1, BLOCKS, TILE, 128), F32),
                *halo_scratch(),
                *tap_scratch,
            ],
            10**9,
            smem=(3,),
        )

    rows, field_grad = reduce_and_exchange(keep_rows, send_rows, outs[4:], finish)
    grads = call(
        unpack_kernel,
        (rows,),
        [
            jax.ShapeDtypeStruct(shape, F32)
            for shape in ((TAPS, C), (1, C), (1, C), (C, HID), (HID,), (C, HID), (1, C))
        ],
        [],
        10**6,
    )
    grad_kernel, gain, shift, grad_in, bias, grad_out, scale = grads
    return (
        block_out.reshape(fields.shape),
        field_grad.reshape(fields.shape),
        grad_kernel,
        gain.reshape(-1),
        shift.reshape(-1),
        grad_in,
        bias,
        grad_out.T,
        scale.reshape(-1),
    )


def solution(mesh):
    cells = P("dp", "tiles", None, None)
    in_specs = (cells, P("tiles", None, None), P("tiles", None)) + (P(),) * 7 + (cells,)
    out_specs = (cells, cells) + (P(),) * 7
    return jax.shard_map(shards, mesh=mesh, in_specs=in_specs, out_specs=out_specs, check_vma=False)
```

time: 422 us -> 116 us (0.27); the launches traced: 414 us -> 115 us
  waiting for transfers between devices: 154 us -> 24.9 us
  blocking collectives: 83.9 us -> 0 us
  local copies, waits for them, and re-layouts: 74.2 us -> 3.77 us
  other arithmetic: 35.4 us -> 1.31 us
  Pallas kernels: 0 us -> 26.7 us
  starting transfers between devices: 37.1 us -> 57.6 us
  between operations: 16.9 us -> 1.05 us
  matrix products: 12.6 us -> 0 us
    psum x1 -> x0, waiting for transfers between devices: 146 us -> none  [shards(): lax.psum((grad_kernel_part, grad_gain_part, grad_shift_part, grad_in_part...]
    psum x1 -> x0, blocking collectives: 83.9 us -> none  [shards(): lax.psum((grad_kernel_part, grad_gain_part, grad_shift_part, grad_in_part...]
    pallas_call x0 -> x9, Pallas kernels: none -> 26.7 us  [call(): pl.pallas_call(kernel, out_shape=out_shape, in_specs=[whole(place(n)) for...]
    concatenate x2 -> x0, local copies, waits for them, and re-layouts: 24.7 us -> none  [extend_tiles(): jnp.concatenate([borders] + from_below + from_above + [jnp.zeros_like(bor...]
    reduce_sum x7 -> x0, other arithmetic: 22.2 us -> none  [the longest x5 11.2 us: kernel_grad(): jnp.sum(window.astype(jnp.float32) * back_values, axis=axes_all)]
    ppermute x12 -> x20, starting transfers between devices: 37 us -> 57.6 us  [swap(): lax.ppermute(block, axis, [(i, partner(i)) for i in range(count) if 0 <=...]
    reshape x9 -> x1, local copies, waits for them, and re-layouts: 16.8 us -> 0.01 us  [shards(): row = lambda v: v.reshape(1, -1)]
    ppermute x12 -> x20, waiting for transfers between devices: 8.47 us -> 24.9 us  [swap(): lax.ppermute(block, axis, [(i, partner(i)) for i in range(count) if 0 <=...]
  transfers between devices with their start and end apart: 13 -> 20, of which waited for: 2 -> 11; matrix products, arithmetic and copies ran while one was open for 12% -> 1% of each run, Pallas kernels for 0% -> 7%
where the time goes in v1:
time: 116 us; the launch traced here: 115 us
  starting transfers between devices  57.6 us (50%)
  Pallas kernels  26.7 us (23%)
  waiting for transfers between devices  24.9 us (21%)
  local copies, waits for them, and re-layouts  3.77 us (3%)
  other arithmetic  1.31 us (1%)
    ppermute x20, starting transfers between devices, swap(): lax.ppermute(block, axis, [(i, partner(i)) for i in range(count) if 0 <=...  57.6 us
    pallas_call x9, Pallas kernels, call(): pl.pallas_call(kernel, out_shape=out_shape, in_specs=[whole(place(n)) for...  26.7 us
    ppermute x20, waiting for transfers between devices, swap(): lax.ppermute(block, axis, [(i, partner(i)) for i in range(count) if 0 <=...  24.9 us
    unnamed x26, local copies, waits for them, and re-layouts  3.71 us
  transfers between devices with their start and end apart: 20, of which 11 were waited for; matrix products, arithmetic and copies ran while one was open for 1% of the time, Pallas kernels for 7%

profile of v1, /device:TPU:1, one launch (start us, length us, event | category | flops | bytes accessed | tf_op | source)
XLA Modules:
  0.0 115.4 jit_solution(10664432553914164169)
XLA Ops:
  0.7 1.0 copy-done
  3.2 2.2 %collective-permute-start = (bf16[5,80,128]{2,1,0:T(8,128)(2,1)S(1)}, bf16[5,80,128]{2,1,0:T(8,128)(2,1)S(1)}, u32[]{:S(2)}, u32[]{:S(2)}) collective-permute-start(bf16[5,80,128]{2,1,0:T(8,128)(2,1)S(1)} %get-tuple-element.82.early.refs_11_), channel_id=1, source_target_pairs={{0,2},{1,3},{2,0},{3,1},{4,6},{5,7},{6,4},{7,5},{8,10},{9,11},{10,... | collective-permute-start | bytes 307208 | tf_op jit(solution)/shard_map/ppermute | solution.py:525
  6.1 1.4 %collective-permute-done.came_early.refs_15_ = bf16[5,80,128]{2,1,0:T(8,128)(2,1)S(1)} collective-permute-done((bf16[5,80,128]{2,1,0:T(8,128)(2,1)S(1)}, bf16[5,80,128]{2,1,0:T(8,128)(2,1)S(1)}, u32[]{:S(2)}, u32[]{:S(2)}) %collective-permute-start) | collective-permute-done | bytes 102432 | tf_op jit(solution)/shard_map/ppermute | solution.py:525
  7.5 3.8 %collective-permute-start.3 = (bf16[11,80,128]{2,1,0:T(8,128)(2,1)S(1)}, bf16[11,80,128]{2,1,0:T(8,128)(2,1)S(1)}, u32[]{:S(2)}, u32[]{:S(2)}) collective-permute-start(bf16[11,80,128]{2,1,0:T(8,128)(2,1)S(1)} %shard_map.179), channel_id=1, source_target_pairs={{0,1},{1,0},{2,3},{3,2},{4,5},{5,4},{6,7},{7,6},{8,9},{9,8},{10,11... | collective-permute-start | bytes 675848 | tf_op jit(solution)/shard_map/ppermute | solution.py:525
  11.3 6.2 %collective-permute-start.2 = (bf16[1,80,128]{2,1,0:T(8,128)(2,1)S(1)}, bf16[1,80,128]{2,1,0:T(8,128)(2,1)S(1)}, u32[]{:S(2)}, u32[]{:S(2)}) collective-permute-start(bf16[1,80,128]{2,1,0:T(8,128)(2,1)S(1)} %get-tuple-element.86), channel_id=1, source_target_pairs={{1,4},{3,6},{4,1},{5,8},{6,3},{7,10},{8,5},{9,12},{10,7},{11,14},{... | collective-permute-start | bytes 61448 | tf_op jit(solution)/shard_map/ppermute | solution.py:525
  17.5 1.4 %collective-permute-done.2.refs_17_ = bf16[1,80,128]{2,1,0:T(8,128)(2,1)S(1)} collective-permute-done((bf16[1,80,128]{2,1,0:T(8,128)(2,1)S(1)}, bf16[1,80,128]{2,1,0:T(8,128)(2,1)S(1)}, u32[]{:S(2)}, u32[]{:S(2)}) %collective-permute-start.2) | collective-permute-done | bytes 20512 | tf_op jit(solution)/shard_map/ppermute | solution.py:525
  20.9 17.1 %shard_map.180 = (bf16[4,16,3072]{2,1,0:T(8,128)(2,1)}, bf16[4,16,3072]{2,1,0:T(8,128)(2,1)S(1)}, f32[1216,128]{1,0:T(8,128)S(1)}, bf16[1216,128]{1,0:T(8,128)(2...) custom-call(bf16[4,16,3072]{2,1,0:T(8,128)(2,1)S(1)} %bitcast.14, ...), custom_call_target="tpu_custom_call" | custom-call | flops 2000000000 | bytes 4000000 | tf_op jit(solution)/shard_map/pallas_call | solution.py:502
  38.1 2.7 %collective-permute-start.5 = (bf16[5,80,128]{2,1,0:T(8,128)(2,1)S(1)}, bf16[5,80,128]{2,1,0:T(8,128)(2,1)S(1)}, u32[]{:S(2)}, u32[]{:S(2)}) collective-permute-start(bf16[5,80,128]{2,1,0:T(8,128)(2,1)S(1)} %get-tuple-element.138.early.refs_5_), channel_id=1, source_target_pairs={{0,2},{1,3},{2,0},{3,1},{4,6},{5,7},{6,4},{7,5},{8,10},{9,11},{10,... | collective-permute-start | bytes 307208 | tf_op jit(solution)/shard_map/ppermute | solution.py:525
  40.8 2.9 %collective-permute-done.5.came_early.refs_9_ = bf16[5,80,128]{2,1,0:T(8,128)(2,1)S(1)} collective-permute-done((bf16[5,80,128]{2,1,0:T(8,128)(2,1)S(1)}, bf16[5,80,128]{2,1,0:T(8,128)(2,1)S(1)}, u32[]{:S(2)}, u32[]{:S(2)}) %collective-permute-start.5) | collective-permute-done | bytes 102432 | tf_op jit(solution)/shard_map/ppermute | solution.py:525
  45.2 3.4 %collective-permute-done.6 = bf16[608,128]{1,0:T(8,128)(2,1)S(1)} collective-permute-done((bf16[608,128]{1,0:T(8,128)(2,1)S(1)}, bf16[608,128]{1,0:T(8,128)(2,1)S(1)}, u32[]{:S(2)}, u32[]{:S(2)}) %collective-permute-start.6) | collective-permute-done | bytes 155680 | tf_op jit(solution)/shard_map/ppermute | solution.py:525
  48.6 1.9 %collective-permute-start.9 = (bf16[11,80,128]{2,1,0:T(8,128)(2,1)S(1)}, bf16[11,80,128]{2,1,0:T(8,128)(2,1)S(1)}, u32[]{:S(2)}, u32[]{:S(2)}) collective-permute-start(bf16[11,80,128]{2,1,0:T(8,128)(2,1)S(1)} %shard_map.181), channel_id=1, source_target_pairs={{0,1},{1,0},{2,3},{3,2},{4,5},{5,4},{6,7},{7,6},{8,9},{9,8},{10,11... | collective-permute-start | bytes 675848 | tf_op jit(solution)/shard_map/ppermute | solution.py:525
  50.5 1.9 %collective-permute-start.8 = (bf16[304,128]{1,0:T(8,128)(2,1)S(1)}, bf16[304,128]{1,0:T(8,128)(2,1)S(1)}, u32[]{:S(2)}, u32[]{:S(2)}) collective-permute-start(bf16[304,128]{1,0:T(8,128)(2,1)S(1)} %dynamic-slice_convert_fusion.1), channel_id=1, source_target_pairs={{0,192},{64,128},{128,64},{192,0},{1,193},{65,129},{129,65},{193,1... | collective-permute-start | bytes 233480 | tf_op jit(solution)/shard_map/ppermute | solution.py:525
  52.5 3.4 %collective-permute-done.8 = bf16[304,128]{1,0:T(8,128)(2,1)S(1)} collective-permute-done((bf16[304,128]{1,0:T(8,128)(2,1)S(1)}, bf16[304,128]{1,0:T(8,128)(2,1)S(1)}, u32[]{:S(2)}, u32[]{:S(2)}) %collective-permute-start.8) | collective-permute-done | bytes 77856 | tf_op jit(solution)/shard_map/ppermute | solution.py:525
  55.9 4.7 %collective-permute-start.10 = (bf16[152,128]{1,0:T(8,128)(2,1)S(1)}, bf16[152,128]{1,0:T(8,128)(2,1)S(1)}, u32[]{:S(2)}, u32[]{:S(2)}) collective-permute-start(bf16[152,128]{1,0:T(8,128)(2,1)S(1)} %dynamic-slice_convert_fusion.2), channel_id=1, source_target_pairs={{0,2},{1,3},{2,0},{3,1},{4,6},{5,7},{6,4},{7,5},{8,10},{9,11},{10,... | collective-permute-start | bytes 116744 | tf_op jit(solution)/shard_map/ppermute | solution.py:525
  60.6 8.5 %collective-permute-start.11 = (bf16[1,80,128]{2,1,0:T(8,128)(2,1)S(1)}, bf16[1,80,128]{2,1,0:T(8,128)(2,1)S(1)}, u32[]{:S(2)}, u32[]{:S(2)}) collective-permute-start(bf16[1,80,128]{2,1,0:T(8,128)(2,1)S(1)} %get-tuple-element.97), channel_id=1, source_target_pairs={{1,4},{3,6},{4,1},{5,8},{6,3},{7,10},{8,5},{9,12},{10,7},{11,14},{... | collective-permute-start | bytes 61448 | tf_op jit(solution)/shard_map/ppermute | solution.py:525
  69.1 1.4 %collective-permute-done.11.refs_11_ = bf16[1,80,128]{2,1,0:T(8,128)(2,1)S(1)} collective-permute-done((bf16[1,80,128]{2,1,0:T(8,128)(2,1)S(1)}, bf16[1,80,128]{2,1,0:T(8,128)(2,1)S(1)}, u32[]{:S(2)}, u32[]{:S(2)}) %collective-permute-start.11) | collective-permute-done | bytes 20512 | tf_op jit(solution)/shard_map/ppermute | solution.py:525
  70.6 2.2 %collective-permute-start.12 = (bf16[152,128]{1,0:T(8,128)(2,1)S(1)}, bf16[152,128]{1,0:T(8,128)(2,1)S(1)}, u32[]{:S(2)}, u32[]{:S(2)}) collective-permute-start(bf16[152,128]{1,0:T(8,128)(2,1)S(1)} %add_convert_fusion.4), channel_id=1, source_target_pairs={{0,6},{1,7},{2,4},{3,5},{4,2},{5,3},{6,0},{7,1},{8,14},{9,15},{10,... | collective-permute-start | bytes 116744 | tf_op jit(solution)/shard_map/ppermute | solution.py:525
  72.7 2.1 %shard_map.182 = bf16[1,16,3072]{2,1,0:T(8,128)(2,1)S(1)} custom-call(bf16[4,16,3072]{2,1,0:T(8,128)(2,1)S(1)} %get-tuple-element.104.refs_0_, bf16[4,16,3072]{2,1,0:T(8,128)(2,1)S(1)} %bitcast.16, s32[4,16,16]{2,1,0:T(8,128)S(1)} %copy-done.3, s32[4,8]{1,0:T(4,128)S(1)} %copy-done.8, f32[49,192]{1,0:T(8,128)S(1)} %copy-done.7, ...), custom_call_target="tpu_custom_call" | custom-call | flops 1000000000 | bytes 4000000 | tf_op jit(solution)/shard_map/pallas_call | solution.py:502
  74.8 1.9 %collective-permute-start.13 = (bf16[152,128]{1,0:T(8,128)(2,1)S(1)}, bf16[152,128]{1,0:T(8,128)(2,1)S(1)}, u32[]{:S(2)}, u32[]{:S(2)}) collective-permute-start(bf16[152,128]{1,0:T(8,128)(2,1)S(1)} %add_convert_fusion.3), channel_id=1, source_target_pairs={{0,8},{1,9},{2,10},{3,11},{4,12},{5,13},{6,14},{7,15},{8,0},{9,1},... | collective-permute-start | bytes 116744 | tf_op jit(solution)/shard_map/ppermute | solution.py:525
  76.7 1.9 %shard_map.183 = bf16[1,16,3072]{2,1,0:T(8,128)(2,1)S(1)} custom-call(bf16[4,16,3072]{2,1,0:T(8,128)(2,1)S(1)} %get-tuple-element.104.refs_0_, bf16[4,16,3072]{2,1,0:T(8,128)(2,1)S(1)} %bitcast.17, s32[4,16,16]{2,1,0:T(8,128)S(1)} %copy-done.3, s32[4,8]{1,0:T(4,128)S(1)} %copy-done.8, f32[49,192]{1,0:T(8,128)S(1)} %copy-done.7, ...), custom_call_target="tpu_custom_call" | custom-call | flops 1000000000 | bytes 4000000 | tf_op jit(solution)/shard_map/pallas_call | solution.py:502
  78.7 8.4 %collective-permute-start.14 = (bf16[152,128]{1,0:T(8,128)(2,1)S(1)}, bf16[152,128]{1,0:T(8,128)(2,1)S(1)}, u32[]{:S(2)}, u32[]{:S(2)}) collective-permute-start(bf16[152,128]{1,0:T(8,128)(2,1)S(1)} %add_convert_fusion.2), channel_id=1, source_target_pairs={{0,24},{1,25},{2,26},{3,27},{4,28},{5,29},{6,30},{7,31},{8,16},{9,... | collective-permute-start | bytes 116744 | tf_op jit(solution)/shard_map/ppermute | solution.py:525
  87.1 1.9 %shard_map.184 = bf16[1,16,3072]{2,1,0:T(8,128)(2,1)S(1)} custom-call(bf16[4,16,3072]{2,1,0:T(8,128)(2,1)S(1)} %get-tuple-element.104.refs_0_, bf16[4,16,3072]{2,1,0:T(8,128)(2,1)S(1)} %bitcast.18, s32[4,16,16]{2,1,0:T(8,128)S(1)} %copy-done.3, s32[4,8]{1,0:T(4,128)S(1)} %copy-done.8, f32[49,192]{1,0:T(8,128)S(1)} %copy-done.7, ...), custom_call_target="tpu_custom_call" | custom-call | flops 1000000000 | bytes 4000000 | tf_op jit(solution)/shard_map/pallas_call | solution.py:502
  89.0 1.0 collective-permute-start.15
  90.0 1.9 %shard_map.185 = bf16[1,16,3072]{2,1,0:T(8,128)(2,1)S(1)} custom-call(bf16[4,16,3072]{2,1,0:T(8,128)(2,1)S(1)} %get-tuple-element.104.refs_0_, bf16[4,16,3072]{2,1,0:T(8,128)(2,1)S(1)} %bitcast.19, s32[4,16,16]{2,1,0:T(8,128)S(1)} %copy-done.3, s32[4,8]{1,0:T(4,128)S(1)} %copy-done.8, f32[49,192]{1,0:T(8,128)S(1)} %copy-done.7, ...), custom_call_target="tpu_custom_call" | custom-call | flops 1000000000 | bytes 4000000 | tf_op jit(solution)/shard_map/pallas_call | solution.py:502
  92.0 1.6 %collective-permute-done.15 = bf16[152,128]{1,0:T(8,128)(2,1)S(1)} collective-permute-done((bf16[152,128]{1,0:T(8,128)(2,1)S(1)}, bf16[152,128]{1,0:T(8,128)(2,1)S(1)}, u32[]{:S(2)}, u32[]{:S(2)}) %collective-permute-start.15) | collective-permute-done | bytes 38944 | tf_op jit(solution)/shard_map/ppermute | solution.py:525
  93.6 1.0 collective-permute-start.16
  94.5 2.2 %collective-permute-done.16 = bf16[152,128]{1,0:T(8,128)(2,1)S(1)} collective-permute-done((bf16[152,128]{1,0:T(8,128)(2,1)S(1)}, bf16[152,128]{1,0:T(8,128)(2,1)S(1)}, u32[]{:S(2)}, u32[]{:S(2)}) %collective-permute-start.16) | collective-permute-done | bytes 38944 | tf_op jit(solution)/shard_map/ppermute | solution.py:525
  96.8 1.9 %collective-permute-start.17 = (bf16[304,128]{1,0:T(8,128)(2,1)S(1)}, bf16[304,128]{1,0:T(8,128)(2,1)S(1)}, u32[]{:S(2)}, u32[]{:S(2)}) collective-permute-start(bf16[304,128]{1,0:T(8,128)(2,1)S(1)} %maximum_select_fusion.3), channel_id=1, source_target_pairs={{0,192},{64,128},{128,64},{192,0},{1,193},{65,129},{129,65},{193,1... | collective-permute-start | bytes 233480 | tf_op jit(solution)/shard_map/ppermute | solution.py:525
  98.7 2.6 %collective-permute-done.17 = bf16[304,128]{1,0:T(8,128)(2,1)S(1)} collective-permute-done((bf16[304,128]{1,0:T(8,128)(2,1)S(1)}, bf16[304,128]{1,0:T(8,128)(2,1)S(1)}, u32[]{:S(2)}, u32[]{:S(2)}) %collective-permute-start.17) | collective-permute-done | bytes 77856 | tf_op jit(solution)/shard_map/ppermute | solution.py:525
  101.5 4.1 %collective-permute-done.18 = bf16[608,128]{1,0:T(8,128)(2,1)S(1)} collective-permute-done((bf16[608,128]{1,0:T(8,128)(2,1)S(1)}, bf16[608,128]{1,0:T(8,128)(2,1)S(1)}, u32[]{:S(2)}, u32[]{:S(2)}) %collective-permute-start.18) | collective-permute-done | bytes 155680 | tf_op jit(solution)/shard_map/ppermute | solution.py:525
  105.7 7.2 %collective-permute-start.19 = (bf16[1216,128]{1,0:T(8,128)(2,1)S(1)}, bf16[1216,128]{1,0:T(8,128)(2,1)S(1)}, u32[]{:S(2)}, u32[]{:S(2)}) collective-permute-start(bf16[1216,128]{1,0:T(8,128)(2,1)S(1)} %maximum_select_fusion.1), channel_id=1, source_target_pairs={{0,1},{1,0},{2,3},{3,2},{4,5},{5,4},{6,7},{7,6},{8,9},{9,8},{10,11... | collective-permute-start | bytes 933896 | tf_op jit(solution)/shard_map/ppermute | solution.py:525
  114.3 1.1 shard_map.186
  (60 shorter events, 7.4 us)
Async XLA Ops:
  0.6 18.3 %copy-start.9 = (f32[192]{0:T(256)S(1)}, f32[192]{0:T(256)}, u32[]{:S(2)}) copy-start(f32[192]{0:T(256)} %param.15) | copy-start | bytes 2308
  0.7 1.0 copy-start
  2.4 15.0 %copy-start.12 = (f32[768]{0:T(1024)S(1)}, f32[768]{0:T(1024)}, u32[]{:S(2)}) copy-start(f32[768]{0:T(1024)} %param.18) | copy-start | bytes 9220
  2.4 16.5 %copy-start.1 = (bf16[1,4,16,3072]{3,2,1,0:T(8,128)(2,1)S(1)}, bf16[1,4,16,3072]{3,2,1,0:T(8,128)(2,1)}, u32[]{:S(2)}) copy-start(bf16[1,4,16,3072]{3,2,1,0:T(8,128)(2,1)} %param.11) | copy-start | bytes 1179652
  2.4 16.5 %copy-start.3 = (s32[4,16,16]{2,1,0:T(8,128)S(1)}, s32[4,16,16]{2,1,0:T(8,128)}, u32[]{:S(2)}) copy-start(s32[4,16,16]{2,1,0:T(8,128)} %refs_2_.9) | copy-start | bytes 12292
  2.4 16.5 %copy-start.4 = (bf16[1,4,16,3072]{3,2,1,0:T(8,128)(2,1)S(1)}, bf16[1,4,16,3072]{3,2,1,0:T(8,128)(2,1)}, u32[]{:S(2)}) copy-start(bf16[1,4,16,3072]{3,2,1,0:T(8,128)(2,1)} %param.21) | copy-start | bytes 1179652
  2.4 16.5 %copy-start.7 = (f32[49,192]{1,0:T(8,128)S(1)}, f32[49,192]{1,0:T(8,128)}, u32[]{:S(2)}) copy-start(f32[49,192]{1,0:T(8,128)} %refs_4_.9) | copy-start | bytes 112900
  2.4 16.5 %copy-start.8 = (s32[4,8]{1,0:T(4,128)S(1)}, s32[4,8]{1,0:T(4,128)}, u32[]{:S(2)}) copy-start(s32[4,8]{1,0:T(4,128)} %refs_3_.9) | copy-start | bytes 388
  2.4 16.5 %copy-start.10 = (f32[192]{0:T(256)S(1)}, f32[192]{0:T(256)}, u32[]{:S(2)}) copy-start(f32[192]{0:T(256)} %param.16) | copy-start | bytes 2308
  2.5 16.5 %copy-start.11 = (f32[192]{0:T(256)S(1)}, f32[192]{0:T(256)}, u32[]{:S(2)}) copy-start(f32[192]{0:T(256)} %param.20) | copy-start | bytes 2308
  3.2 4.3 %collective-permute-start = (bf16[5,80,128]{2,1,0:T(8,128)(2,1)S(1)}, bf16[5,80,128]{2,1,0:T(8,128)(2,1)S(1)}, u32[]{:S(2)}, u32[]{:S(2)}) collective-permute-start(bf16[5,80,128]{2,1,0:T(8,128)(2,1)S(1)} %get-tuple-element.82.early.refs_11_), channel_id=1, source_target_pairs={{0,2},{1,3},{2,0},{3,1},{4,6},{5,7},{6,4},{7,5},{8,10},{9,11},{10,... | collective-permute-start | bytes 307208 | tf_op jit(solution)/shard_map/ppermute | solution.py:525
  5.4 2.1 %collective-permute-start.1 = (bf16[5,80,128]{2,1,0:T(8,128)(2,1)S(1)}, bf16[5,80,128]{2,1,0:T(8,128)(2,1)S(1)}, u32[]{:S(2)}, u32[]{:S(2)}) collective-permute-start(bf16[5,80,128]{2,1,0:T(8,128)(2,1)S(1)} %get-tuple-element.83.late.refs_12_), channel_id=1, source_target_pairs={{2,4},{3,5},{4,2},{5,3},{6,8},{7,9},{8,6},{9,7},{10,12},{11,13},{1... | collective-permute-start | bytes 307208 | tf_op jit(solution)/shard_map/ppermute | solution.py:525
  7.5 11.4 %collective-permute-start.3 = (bf16[11,80,128]{2,1,0:T(8,128)(2,1)S(1)}, bf16[11,80,128]{2,1,0:T(8,128)(2,1)S(1)}, u32[]{:S(2)}, u32[]{:S(2)}) collective-permute-start(bf16[11,80,128]{2,1,0:T(8,128)(2,1)S(1)} %shard_map.179), channel_id=1, source_target_pairs={{0,1},{1,0},{2,3},{3,2},{4,5},{5,4},{6,7},{7,6},{8,9},{9,8},{10,11... | collective-permute-start | bytes 675848 | tf_op jit(solution)/shard_map/ppermute | solution.py:525
  11.3 7.6 %collective-permute-start.2 = (bf16[1,80,128]{2,1,0:T(8,128)(2,1)S(1)}, bf16[1,80,128]{2,1,0:T(8,128)(2,1)S(1)}, u32[]{:S(2)}, u32[]{:S(2)}) collective-permute-start(bf16[1,80,128]{2,1,0:T(8,128)(2,1)S(1)} %get-tuple-element.86), channel_id=1, source_target_pairs={{1,4},{3,6},{4,1},{5,8},{6,3},{7,10},{8,5},{9,12},{10,7},{11,14},{... | collective-permute-start | bytes 61448 | tf_op jit(solution)/shard_map/ppermute | solution.py:525
  19.0 1.0 copy-start.5
  19.9 1.0 copy-start.6
  38.0 5.7 %collective-permute-start.4 = (bf16[1216,128]{1,0:T(8,128)(2,1)S(1)}, bf16[1216,128]{1,0:T(8,128)(2,1)S(1)}, u32[]{:S(2)}, u32[]{:S(2)}) collective-permute-start(bf16[1216,128]{1,0:T(8,128)(2,1)S(1)} %get-tuple-element.89), channel_id=1, source_target_pairs={{0,1},{1,0},{2,3},{3,2},{4,5},{5,4},{6,7},{7,6},{8,9},{9,8},{10,11... | collective-permute-start | bytes 933896 | tf_op jit(solution)/shard_map/ppermute | solution.py:525
  38.1 5.6 %collective-permute-start.5 = (bf16[5,80,128]{2,1,0:T(8,128)(2,1)S(1)}, bf16[5,80,128]{2,1,0:T(8,128)(2,1)S(1)}, u32[]{:S(2)}, u32[]{:S(2)}) collective-permute-start(bf16[5,80,128]{2,1,0:T(8,128)(2,1)S(1)} %get-tuple-element.138.early.refs_5_), channel_id=1, source_target_pairs={{0,2},{1,3},{2,0},{3,1},{4,6},{5,7},{6,4},{7,5},{8,10},{9,11},{10,... | collective-permute-start | bytes 307208 | tf_op jit(solution)/shard_map/ppermute | solution.py:525
  43.8 4.7 %collective-permute-start.6 = (bf16[608,128]{1,0:T(8,128)(2,1)S(1)}, bf16[608,128]{1,0:T(8,128)(2,1)S(1)}, u32[]{:S(2)}, u32[]{:S(2)}) collective-permute-start(bf16[608,128]{1,0:T(8,128)(2,1)S(1)} %dynamic-slice_convert_fusion), channel_id=1, source_target_pairs={{0,64},{64,0},{128,192},{192,128},{1,65},{65,1},{129,193},{193,129... | collective-permute-start | bytes 466952 | tf_op jit(solution)/shard_map/ppermute | solution.py:525
  44.5 0.7 collective-permute-start.7
  48.6 7.2 %collective-permute-start.9 = (bf16[11,80,128]{2,1,0:T(8,128)(2,1)S(1)}, bf16[11,80,128]{2,1,0:T(8,128)(2,1)S(1)}, u32[]{:S(2)}, u32[]{:S(2)}) collective-permute-start(bf16[11,80,128]{2,1,0:T(8,128)(2,1)S(1)} %shard_map.181), channel_id=1, source_target_pairs={{0,1},{1,0},{2,3},{3,2},{4,5},{5,4},{6,7},{7,6},{8,9},{9,8},{10,11... | collective-permute-start | bytes 675848 | tf_op jit(solution)/shard_map/ppermute | solution.py:525
  50.5 5.3 %collective-permute-start.8 = (bf16[304,128]{1,0:T(8,128)(2,1)S(1)}, bf16[304,128]{1,0:T(8,128)(2,1)S(1)}, u32[]{:S(2)}, u32[]{:S(2)}) collective-permute-start(bf16[304,128]{1,0:T(8,128)(2,1)S(1)} %dynamic-slice_convert_fusion.1), channel_id=1, source_target_pairs={{0,192},{64,128},{128,64},{192,0},{1,193},{65,129},{129,65},{193,1... | collective-permute-start | bytes 233480 | tf_op jit(solution)/shard_map/ppermute | solution.py:525
  55.9 14.7 %collective-permute-start.10 = (bf16[152,128]{1,0:T(8,128)(2,1)S(1)}, bf16[152,128]{1,0:T(8,128)(2,1)S(1)}, u32[]{:S(2)}, u32[]{:S(2)}) collective-permute-start(bf16[152,128]{1,0:T(8,128)(2,1)S(1)} %dynamic-slice_convert_fusion.2), channel_id=1, source_target_pairs={{0,2},{1,3},{2,0},{3,1},{4,6},{5,7},{6,4},{7,5},{8,10},{9,11},{10,... | collective-permute-start | bytes 116744 | tf_op jit(solution)/shard_map/ppermute | solution.py:525
  60.6 9.9 %collective-permute-start.11 = (bf16[1,80,128]{2,1,0:T(8,128)(2,1)S(1)}, bf16[1,80,128]{2,1,0:T(8,128)(2,1)S(1)}, u32[]{:S(2)}, u32[]{:S(2)}) collective-permute-start(bf16[1,80,128]{2,1,0:T(8,128)(2,1)S(1)} %get-tuple-element.97), channel_id=1, source_target_pairs={{1,4},{3,6},{4,1},{5,8},{6,3},{7,10},{8,5},{9,12},{10,7},{11,14},{... | collective-permute-start | bytes 61448 | tf_op jit(solution)/shard_map/ppermute | solution.py:525
  70.6 4.3 %collective-permute-start.12 = (bf16[152,128]{1,0:T(8,128)(2,1)S(1)}, bf16[152,128]{1,0:T(8,128)(2,1)S(1)}, u32[]{:S(2)}, u32[]{:S(2)}) collective-permute-start(bf16[152,128]{1,0:T(8,128)(2,1)S(1)} %add_convert_fusion.4), channel_id=1, source_target_pairs={{0,6},{1,7},{2,4},{3,5},{4,2},{5,3},{6,0},{7,1},{8,14},{9,15},{10,... | collective-permute-start | bytes 116744 | tf_op jit(solution)/shard_map/ppermute | solution.py:525
  74.8 3.8 %collective-permute-start.13 = (bf16[152,128]{1,0:T(8,128)(2,1)S(1)}, bf16[152,128]{1,0:T(8,128)(2,1)S(1)}, u32[]{:S(2)}, u32[]{:S(2)}) collective-permute-start(bf16[152,128]{1,0:T(8,128)(2,1)S(1)} %add_convert_fusion.3), channel_id=1, source_target_pairs={{0,8},{1,9},{2,10},{3,11},{4,12},{5,13},{6,14},{7,15},{8,0},{9,1},... | collective-permute-start | bytes 116744 | tf_op jit(solution)/shard_map/ppermute | solution.py:525
  78.7 10.3 %collective-permute-start.14 = (bf16[152,128]{1,0:T(8,128)(2,1)S(1)}, bf16[152,128]{1,0:T(8,128)(2,1)S(1)}, u32[]{:S(2)}, u32[]{:S(2)}) collective-permute-start(bf16[152,128]{1,0:T(8,128)(2,1)S(1)} %add_convert_fusion.2), channel_id=1, source_target_pairs={{0,24},{1,25},{2,26},{3,27},{4,28},{5,29},{6,30},{7,31},{8,16},{9,... | collective-permute-start | bytes 116744 | tf_op jit(solution)/shard_map/ppermute | solution.py:525
  89.0 4.5 %collective-permute-start.15 = (bf16[152,128]{1,0:T(8,128)(2,1)S(1)}, bf16[152,128]{1,0:T(8,128)(2,1)S(1)}, u32[]{:S(2)}, u32[]{:S(2)}) collective-permute-start(bf16[152,128]{1,0:T(8,128)(2,1)S(1)} %add_convert_fusion.1), channel_id=1, source_target_pairs={{0,56},{1,57},{2,58},{3,59},{4,60},{5,61},{6,62},{7,63},{8,48},{9,... | collective-permute-start | bytes 116744 | tf_op jit(solution)/shard_map/ppermute | solution.py:525
  93.6 3.2 %collective-permute-start.16 = (bf16[152,128]{1,0:T(8,128)(2,1)S(1)}, bf16[152,128]{1,0:T(8,128)(2,1)S(1)}, u32[]{:S(2)}, u32[]{:S(2)}) collective-permute-start(bf16[152,128]{1,0:T(8,128)(2,1)S(1)} %add_convert_fusion), channel_id=1, source_target_pairs={{0,2},{1,3},{2,0},{3,1},{4,6},{5,7},{6,4},{7,5},{8,10},{9,11},{10,... | collective-permute-start | bytes 116744 | tf_op jit(solution)/shard_map/ppermute | solution.py:525
  96.8 4.5 %collective-permute-start.17 = (bf16[304,128]{1,0:T(8,128)(2,1)S(1)}, bf16[304,128]{1,0:T(8,128)(2,1)S(1)}, u32[]{:S(2)}, u32[]{:S(2)}) collective-permute-start(bf16[304,128]{1,0:T(8,128)(2,1)S(1)} %maximum_select_fusion.3), channel_id=1, source_target_pairs={{0,192},{64,128},{128,64},{192,0},{1,193},{65,129},{129,65},{193,1... | collective-permute-start | bytes 233480 | tf_op jit(solution)/shard_map/ppermute | solution.py:525
  101.4 4.2 %collective-permute-start.18 = (bf16[608,128]{1,0:T(8,128)(2,1)S(1)}, bf16[608,128]{1,0:T(8,128)(2,1)S(1)}, u32[]{:S(2)}, u32[]{:S(2)}) collective-permute-start(bf16[608,128]{1,0:T(8,128)(2,1)S(1)} %maximum_select_fusion.2), channel_id=1, source_target_pairs={{0,64},{64,0},{128,192},{192,128},{1,65},{65,1},{129,193},{193,129... | collective-permute-start | bytes 466952 | tf_op jit(solution)/shard_map/ppermute | solution.py:525
  105.7 8.4 %collective-permute-start.19 = (bf16[1216,128]{1,0:T(8,128)(2,1)S(1)}, bf16[1216,128]{1,0:T(8,128)(2,1)S(1)}, u32[]{:S(2)}, u32[]{:S(2)}) collective-permute-start(bf16[1216,128]{1,0:T(8,128)(2,1)S(1)} %maximum_select_fusion.1), channel_id=1, source_target_pairs={{0,1},{1,0},{2,3},{3,2},{4,5},{5,4},{6,7},{7,6},{8,9},{9,8},{10,11... | collective-permute-start | bytes 933896 | tf_op jit(solution)/shard_map/ppermute | solution.py:525
  (1 other events, 0.8 us)

commit v2 on v1

--- a/solution.py
+++ b/solution.py
@@ -40,7 +40,7 @@
     return jnp.dot(keep, spread, preferred_element_type=F32)
 
 
-def chip_is_even():
+def up_comes_first():
     return lax.rem(lax.div(lax.axis_index("tiles"), 2), 2) == 0
 
 
@@ -49,7 +49,7 @@
 
 
 def emit_strips(tile_block, strip, early, late, far, right_own, left_own):
-    even, first_core = chip_is_even(), core_is_first()
+    even, first_core = up_comes_first(), core_is_first()
     higher, lower = jnp.where(even, 0, 1), jnp.where(even, 1, 0)
 
     def put(place, entry, rows, values):
@@ -103,7 +103,7 @@
 
 
 def by_chip(early, late, came_early, came_late, work):
-    even = chip_is_even()
+    even = up_comes_first()
 
     @pl.when(even)
     def _():
@@ -313,16 +313,8 @@
     return lax.dot_general(left, right, (((0,), (0,)), ((), ())), preferred_element_type=F32)
 
 
-def prepare_kernel(fields_far, mask_far, *refs):
-    strips, (blocks, strip, fields, mask, sems) = refs[0:5], refs[5:]
-    copies = [
-        pltpu.make_async_copy(fields_far, fields, sems.at[0]),
-        pltpu.make_async_copy(mask_far, mask, sems.at[1]),
-    ]
-    for copy in copies:
-        copy.start()
-    for copy in copies:
-        copy.wait()
+def prepare_kernel(fields, mask, *refs):
+    strips, (blocks, strip) = refs[0:5], refs[5:]
     for s in range(TPD):
         keep = expand_mask(mask, s) > 0.5
         values = jnp.where(keep, fields[s].astype(F32), 0.0)
@@ -332,20 +324,16 @@
 
 
 def block_kernel(*refs):
-    fields, cotangent, mask, near, dw, gain_ref, bias_ref, w_in_far, b_in, w_out_far, scale_ref = refs[0:11]
-    given = refs[11:19]
-    block_out, back_out, keep_rows, send_rows = refs[19:23]
-    strips = refs[23:28]
+    fields, cotangent, mask, near, dw, gain_ref, bias_ref, weights, b_in, scale_ref = refs[0:10]
+    given = refs[10:18]
+    block_out, back_out, keep_rows, send_rows = refs[18:22]
+    strips = refs[22:27]
+    w_in, w_out = weights.at[0:C], weights.at[C : 2 * C]
     (
         padded, shifted_pad, keep_blocks, blocks, strip, rows_below, rows_above, right_cols, left_cols,
-        wide, taps, rows_a, rows_b, norm_rows, hid_rows, bb_rows, pre_rows, sums, bias_sums, extra,
-        w_in, w_out, weight_sems,
-    ) = refs[28:]
-
-    arrive_in = pltpu.make_async_copy(w_in_far, w_in, weight_sems.at[0])
-    arrive_out = pltpu.make_async_copy(w_out_far, w_out, weight_sems.at[1])
-    arrive_in.start()
-    arrive_out.start()
+        wide, taps, rows_a_all, rows_b_all, norm_rows, hid_rows, bb_rows, pre_rows, sums, bias_sums, extra,
+    ) = refs[27:]
+
     for s in range(TPD):
         keep = expand_mask(mask, s)
         values = jnp.where(keep > 0.5, fields[s].astype(F32), 0.0)
@@ -357,13 +345,12 @@
     edges = (rows_below, rows_above, right_cols, left_cols)
     fill_halo(padded, shifted_pad, near, strip, edges, range(TPD))
     depthwise(padded, shifted_pad, taps, blocks, False)
-    arrive_in.wait()
-    arrive_out.wait()
 
     sums[...] = jnp.zeros_like(sums)
     bias_sums[...] = jnp.zeros_like(bias_sums)
 
     def one_tile(s, carry):
+        rows_a, rows_b = rows_a_all.at[s], rows_b_all.at[s]
         gain, scale = gain_ref[...], scale_ref[...]
         to_rows(lambda t: blocks[s, t], rows_a)
         to_rows(
@@ -378,7 +365,9 @@
         norm_rows[s] = shifted
         preact = jnp.dot(shifted, w_in[...], preferred_element_type=F32) + b_in[...]
         bell = jnp.exp(-0.5 * preact * preact)
-        u = 1.0 / (1.0 + (0.3275911 * INV_SQRT2) * jnp.abs(preact))
+        below = 1.0 + (0.3275911 * INV_SQRT2) * jnp.abs(preact)
+        u = pl.reciprocal(below, approx=True)
+        u = u * (2.0 - below * u)
         series = u * (
             0.5 * 0.254829592
             + u * (0.5 * -0.284496736 + u * (0.5 * 1.421413741 + u * (0.5 * -1.453152027 + u * (0.5 * 1.061405429))))
@@ -420,7 +409,7 @@
         from_rows(rows_b, put_back)
         return carry
 
-    lax.fori_loop(0, TPD, one_tile, 0)
+    lax.fori_loop(0, TPD, one_tile, 0, unroll=True)
 
     emit_strips(lambda s, t, row, rows: blocks[s, t, row : row + rows, :], strip, *strips)
     kernel_grad(padded, shifted_pad, blocks, wide)
@@ -497,12 +486,11 @@
     return pl.BlockSpec(memory_space=memory)
 
 
-def call(kernel, inputs, out_shape, scratch, cost, smem=(), far=()):
-    place = lambda n: pltpu.SMEM if n in smem else pl.ANY if n in far else pltpu.VMEM
+def call(kernel, inputs, out_shape, scratch, cost, smem=()):
     return pl.pallas_call(
         kernel,
         out_shape=out_shape,
-        in_specs=[whole(place(n)) for n in range(len(inputs))],
+        in_specs=[whole(pltpu.SMEM if n in smem else pltpu.VMEM) for n in range(len(inputs))],
         out_specs=jax.tree.map(lambda _: whole(), out_shape),
         scratch_shapes=scratch,
         compiler_params=pltpu.CompilerParams(vmem_limit_bytes=VMEM_LIMIT),
@@ -521,20 +509,21 @@
 
 
 def swap(block, axis, partner):
-    count = lax.axis_size(axis)
-    return lax.ppermute(block, axis, [(i, partner(i)) for i in range(count) if 0 <= partner(i) < count])
-
-
-def chip_up(i):
+    return lax.ppermute(block, axis, [(i, partner(i)) for i in range(lax.axis_size(axis))])
+
+
+def first_chip(i):
     return i ^ 2
 
 
-def chip_down(i):
-    return ((i // 2 + 1) ^ 1) * 2 - 2 + i % 2
+def second_chip(i):
+    j = ((i // 2 + 1) ^ 1) * 2 - 2 + i % 2
+    return j if 0 <= j < lax.axis_size("tiles") else i ^ 1
 
 
 def three_away(i):
-    return i + 3 if i % 2 else i - 3
+    j = i + 3 if i % 2 else i - 3
+    return j if 0 <= j < lax.axis_size("tiles") else i ^ 2
 
 
 def other_core(i):
@@ -548,50 +537,83 @@
 
 def exchange_strips(strips):
     early, late, far, right_own, left_own = strips
-    came_early = swap(early, "tiles", chip_up)
-    came_late = swap(late, "tiles", chip_down)
     came_far = swap(far, "tiles", three_away)
+    came_early = swap(early, "tiles", first_chip)
+    came_late = swap(late, "tiles", second_chip)
+    came_far, came_early, came_late = lax.optimization_barrier((came_far, came_early, came_late))
     passed = swap(relay(early, late, came_early, came_late), "tiles", other_core)
     return (early, late, right_own, left_own, came_early, came_late, came_far, passed)
 
 
+MOVES = {"x1": (1, 0), "x2": (3, 0), "y1": (0, 2), "y2": (0, 6), "z1": (0, 8), "z2": (0, 24), "z3": (0, 56)}
+ORDERS = (("x1", "x2", "y1", "y2", "z1", "z2", "z3"), ("y1", "y2", "x1", "x2", "z1", "z2", "z3"))
+
+
+def trade(block, step):
+    samples, tiles = lax.axis_size("dp"), lax.axis_size("tiles")
+    route = []
+    for x in range(samples):
+        for t in range(tiles):
+            over_x, over_t = MOVES[ORDERS[t % 2][step]]
+            route.append((x * tiles + t, (x ^ over_x) * tiles + (t ^ over_t)))
+    return lax.ppermute(block, ("dp", "tiles"), route)
+
+
 def reduce_and_exchange(keep, send, strips, finish):
     early, late, far, right_own, left_own = strips
+    barrier = lax.optimization_barrier
     place = lax.axis_index("tiles")
     core, y = place % 2, (place // 2) % 4
     x = lax.axis_index("dp")
+    at = {"x1": (x + x // 2) % 2, "x2": x // 2, "y1": (y + y // 2) % 2, "y2": y // 2}
+    bits = [jnp.where(core == 0, at[ORDERS[0][n]], at[ORDERS[1][n]]) for n in range(3)]
 
     def halves(block, bit):
         n = block.shape[0] // 2
         own = lax.dynamic_slice_in_dim(block, bit * n, n, 0)
         return own, lax.dynamic_slice_in_dim(block, (1 - bit) * n, n, 0).astype(BF16)
 
-    def join(block, axis, partner, bit):
-        other = swap(block, axis, partner)
+    def join(block, other, bit):
         return jnp.where(bit == 0, jnp.concatenate([block, other], 0), jnp.concatenate([other, block], 0))
 
-    first_x, second_x, first_y = (x + x // 2) % 2, x // 2, (y + y // 2) % 2
-    came, came_early = lax.optimization_barrier((swap(send, "tiles", other_core), swap(early, "tiles", chip_up)))
-    own, other = halves(keep + came.astype(F32), first_x)
-    came, came_late = lax.optimization_barrier((swap(other, "dp", lambda i: i ^ 1), swap(late, "tiles", chip_down)))
-    own, other = halves(own + came.astype(F32), second_x)
+    came_far = swap(far, "tiles", three_away)
+    own, other = halves(keep + swap(send, "tiles", other_core).astype(F32), bits[0])
+    other, early = barrier((other, early))
+    came_early = swap(early, "tiles", first_chip)
+    came, came_far = barrier((trade(other, 0), came_far))
+    own, other = halves(own + came.astype(F32), bits[1])
+    other, late = barrier((other, late))
+    came_late = swap(late, "tiles", second_chip)
+    came, came_early = barrier((trade(other, 1), came_early))
+    own, other = halves(own + came.astype(F32), bits[2])
+    came, came_late = barrier((trade(other, 2), came_late))
+    mine = own + came.astype(F32)
     between = relay(early, late, came_early, came_late)
-    came, passed = lax.optimization_barrier((swap(other, "dp", lambda i: i ^ 3), swap(between, "tiles", other_core)))
-    own, other = halves(own + came.astype(F32), first_y)
-    came, came_far = lax.optimization_barrier((swap(other, "tiles", lambda i: i ^ 2), swap(far, "tiles", three_away)))
-    mine = own + came.astype(F32)
+    sent, between = barrier((mine.astype(BF16), between))
+    passed = swap(between, "tiles", other_core)
+    mine = sent.astype(F32) + trade(sent, 3).astype(F32)
+    sent = mine.astype(BF16)
+    came, passed = barrier((trade(sent, 4), passed))
+    mine = sent.astype(F32) + came.astype(F32)
     given = (early, late, right_own, left_own, came_early, came_late, came_far, passed)
     parts = []
-    for tile, mask in enumerate((6, 8, 24, 56)):
-        sent, given = lax.optimization_barrier((mine.astype(BF16), given))
-        came, part = lax.optimization_barrier((swap(sent, "tiles", lambda i: i ^ mask), finish(tile, given)))
+
+    def beside(sent, step):
+        nonlocal given
+        sent, given = barrier((sent, given))
+        came, part = barrier((trade(sent, step), finish(len(parts), given)))
         parts.append(part)
+        return sent, came
+
+    for step in (5, 6):
+        sent, came = beside(mine.astype(BF16), step)
         mine = sent.astype(F32) + came.astype(F32)
     mine = mine.astype(BF16)
-    mine = join(mine, "tiles", lambda i: i ^ 2, first_y)
-    mine = join(mine, "dp", lambda i: i ^ 3, second_x)
-    mine = join(mine, "dp", lambda i: i ^ 1, first_x)
-    return join(mine, "tiles", other_core, core), jnp.concatenate(parts, 0)
+    for step in (2, 1):
+        mine, came = beside(mine, step)
+        mine = join(mine, came, bits[step])
+    mine = join(mine, trade(mine, 0), bits[0])
+    return join(mine, swap(mine, "tiles", other_core), core), jnp.concatenate(parts, 0)
 
 
 def shards(
@@ -605,25 +627,15 @@
     tap_scratch = [pltpu.VMEM((3, 56, 128), F32), pltpu.VMEM((3 * TAPS, 8, 128), F32)]
 
     strips = call(
-        prepare_kernel,
-        (tiles, ocean_mask),
-        strip_shapes(),
-        [
-            block_scratch,
-            pltpu.VMEM((STRIP, 128), F32),
-            pltpu.VMEM((TPD, TILE, WIDTH), BF16),
-            pltpu.VMEM((TPD, TILE, TILE), jnp.int32),
-            pltpu.SemaphoreType.DMA((2,)),
-        ],
-        10**6,
-        far=(0, 1),
+        prepare_kernel, (tiles, ocean_mask), strip_shapes(), [block_scratch, pltpu.VMEM((STRIP, 128), F32)], 10**6
     )
     given = exchange_strips(strips)
     row = lambda v: v.reshape(1, -1)
+    weights = jnp.concatenate([w_in, w_out.T], 0)
     outs = call(
         block_kernel,
         (
-            tiles, cot, ocean_mask, neighbours, dw_kernel, row(ln_gain), row(ln_bias), w_in, row(b_in), w_out.T,
+            tiles, cot, ocean_mask, neighbours, dw_kernel, row(ln_gain), row(ln_bias), weights, row(b_in),
             row(layer_scale), *given,
         ),
         [
@@ -635,8 +647,8 @@
         ],
         [
             pad_scratch, pad_scratch, block_scratch, block_scratch, *halo_scratch(), *tap_scratch,
-            pltpu.VMEM((CELLS, 256), F32),
-            pltpu.VMEM((CELLS, 256), F32),
+            pltpu.VMEM((TPD, CELLS, 256), F32),
+            pltpu.VMEM((TPD, CELLS, 256), F32),
             pltpu.VMEM((TPD, CELLS, C), BF16),
             pltpu.VMEM((TPD, CELLS, HID), BF16),
             pltpu.VMEM((TPD, CELLS, C), BF16),
@@ -644,13 +656,9 @@
             pltpu.VMEM((8, 256), F32),
             pltpu.VMEM((1, HID), F32),
             pltpu.VMEM((EXTRA, 128), F32),
-            pltpu.VMEM((C, HID), BF16),
-            pltpu.VMEM((C, HID), BF16),
-            pltpu.SemaphoreType.DMA((2,)),
         ],
         2 * 10**9,
         smem=(3,),
-        far=(7, 9),
     )
     block_out, back, keep_rows, send_rows = outs[0:4]
 

time: 116 us -> 92.5 us (0.80)
  starting transfers between devices: 57.6 us -> 44.8 us
  waiting for transfers between devices: 24.9 us -> 17.7 us
  local copies, waits for them, and re-layouts: 3.77 us -> 1.87 us
    ppermute x20, starting transfers between devices: 57.6 us -> 44.8 us  [the longest x10 25 us: swap(): lax.ppermute(block, axis, [(i, partner(i)) for i in range(lax.axis_size(a...]
    ppermute x20, waiting for transfers between devices: 24.9 us -> 17.7 us  [the longest x10 12.3 us: trade(): return lax.ppermute(block, ('dp', 'tiles'), route)]
    unnamed x26, local copies, waits for them, and re-layouts: 3.71 us -> 1.81 us
  transfers between devices with their start and end apart: 20 -> 20, of which waited for: 11 -> 12; matrix products, arithmetic and copies ran while one was open for 1% -> 1% of each run, Pallas kernels for 7% -> 8%
where the time goes in v2:
time: 92.5 us; the launch traced here: 92.4 us
  starting transfers between devices  44.8 us (48%)
  Pallas kernels  25.6 us (28%)
  waiting for transfers between devices  17.7 us (19%)
  local copies, waits for them, and re-layouts  1.87 us (2%)
  other arithmetic  1.35 us (1%)
  between operations  0.97 us (1%)
    pallas_call x9, Pallas kernels, call(): pl.pallas_call(kernel, out_shape=out_shape, in_specs=[whole(pltpu.SMEM if...  25.6 us
    ppermute x10, starting transfers between devices, swap(): lax.ppermute(block, axis, [(i, partner(i)) for i in range(lax.axis_size(a...  25 us
    ppermute x10, starting transfers between devices, trade(): return lax.ppermute(block, ('dp', 'tiles'), route)  19.9 us
    ppermute x10, waiting for transfers between devices, trade(): return lax.ppermute(block, ('dp', 'tiles'), route)  12.3 us
    ppermute x10, waiting for transfers between devices, swap(): lax.ppermute(block, axis, [(i, partner(i)) for i in range(lax.axis_size(a...  5.4 us
  transfers between devices with their start and end apart: 20, of which 12 were waited for; matrix products, arithmetic and copies ran while one was open for 1% of the time, Pallas kernels for 8%

profile of v2, /device:TPU:1, one launch (start us, length us, event | category | flops | bytes accessed | tf_op | source)
XLA Modules:
  0.0 92.4 jit_solution(10136003860318237268)
XLA Ops:
  0.7 1.0 %copy-done = bf16[1,4,16,3072]{3,2,1,0:T(8,128)(2,1)S(1)} copy-done((bf16[1,4,16,3072]{3,2,1,0:T(8,128)(2,1)S(1)}, bf16[1,4,16,3072]{3,2,1,0:T(8,128)(2,1)}, u32[]{:S(2)}) %copy-start) | copy-done | bytes 393240
  1.6 0.8 copy-done.2
  2.9 2.2 %collective-permute-start.1 = (bf16[5,80,128]{2,1,0:T(8,128)(2,1)S(1)}, bf16[5,80,128]{2,1,0:T(8,128)(2,1)S(1)}, u32[]{:S(2)}, u32[]{:S(2)}) collective-permute-start(bf16[5,80,128]{2,1,0:T(8,128)(2,1)S(1)} %get-tuple-element.91.early.refs_10_), channel_id=1, source_target_pairs={{0,2},{1,3},{2,0},{3,1},{4,6},{5,7},{6,4},{7,5},{8,10},{9,11},{10,... | collective-permute-start | bytes 307208 | tf_op jit(solution)/shard_map/ppermute | solution.py:512
  5.1 1.2 %collective-permute-start.2 = (bf16[5,80,128]{2,1,0:T(8,128)(2,1)S(1)}, bf16[5,80,128]{2,1,0:T(8,128)(2,1)S(1)}, u32[]{:S(2)}, u32[]{:S(2)}) collective-permute-start(bf16[5,80,128]{2,1,0:T(8,128)(2,1)S(1)} %get-tuple-element.92.late.refs_11_), channel_id=1, source_target_pairs={{0,1},{1,0},{2,4},{3,5},{4,2},{5,3},{6,8},{7,9},{8,6},{9,7},{10,12... | collective-permute-start | bytes 307208 | tf_op jit(solution)/shard_map/ppermute | solution.py:512
  6.3 3.6 %collective-permute-start = (bf16[1,80,128]{2,1,0:T(8,128)(2,1)S(1)}, bf16[1,80,128]{2,1,0:T(8,128)(2,1)S(1)}, u32[]{:S(2)}, u32[]{:S(2)}) collective-permute-start(bf16[1,80,128]{2,1,0:T(8,128)(2,1)S(1)} %get-tuple-element.95), channel_id=1, source_target_pairs={{0,2},{1,4},{2,0},{3,6},{4,1},{5,8},{6,3},{7,10},{8,5},{9,12},{10,... | collective-permute-start | bytes 61448 | tf_op jit(solution)/shard_map/ppermute | solution.py:512
  9.9 1.5 %collective-permute-done.refs_16_ = bf16[1,80,128]{2,1,0:T(8,128)(2,1)S(1)} collective-permute-done((bf16[1,80,128]{2,1,0:T(8,128)(2,1)S(1)}, bf16[1,80,128]{2,1,0:T(8,128)(2,1)S(1)}, u32[]{:S(2)}, u32[]{:S(2)}) %collective-permute-start) | collective-permute-done | bytes 20512 | tf_op jit(solution)/shard_map/ppermute | solution.py:512
  11.7 1.4 %collective-permute-done.3.refs_17_ = bf16[11,80,128]{2,1,0:T(8,128)(2,1)S(1)} collective-permute-done((bf16[11,80,128]{2,1,0:T(8,128)(2,1)S(1)}, bf16[11,80,128]{2,1,0:T(8,128)(2,1)S(1)}, u32[]{:S(2)}, u32[]{:S(2)}) %collective-permute-start.3) | collective-permute-done | bytes 225312 | tf_op jit(solution)/shard_map/ppermute | solution.py:512
  13.1 16.2 %shard_map.180 = (bf16[4,16,3072]{2,1,0:T(8,128)(2,1)}, bf16[4,16,3072]{2,1,0:T(8,128)(2,1)S(1)}, f32[1216,128]{1,0:T(8,128)S(1)}, bf16[1216,128]{1,0:T(8,128)(2...) custom-call(bf16[4,16,3072]{2,1,0:T(8,128)(2,1)S(1)} %bitcast.14, ...), custom_call_target="tpu_custom_call" | custom-call | flops 2000000000 | bytes 4000000 | tf_op jit(solution)/shard_map/pallas_call | solution.py:490
  29.4 1.5 %collective-permute-done.4 = bf16[1216,128]{1,0:T(8,128)(2,1)S(1)} collective-permute-done((bf16[1216,128]{1,0:T(8,128)(2,1)S(1)}, bf16[1216,128]{1,0:T(8,128)(2,1)S(1)}, u32[]{:S(2)}, u32[]{:S(2)}) %collective-permute-start.4) | collective-permute-done | bytes 311328 | tf_op jit(solution)/shard_map/ppermute | solution.py:512
  31.0 1.0 %collective-permute-start.5 = (bf16[608,128]{1,0:T(8,128)(2,1)S(1)}, bf16[608,128]{1,0:T(8,128)(2,1)S(1)}, u32[]{:S(2)}, u32[]{:S(2)}) collective-permute-start(bf16[608,128]{1,0:T(8,128)(2,1)S(1)} %dynamic-slice_convert_fusion), channel_id=1, source_target_pairs={{0,64},{1,3},{2,66},{3,1},{4,68},{5,7},{6,70},{7,5},{8,72},{9,11},... | collective-permute-start | bytes 466952 | tf_op jit(solution)/shard_map/ppermute | solution.py:559
  32.0 3.8 %collective-permute-start.6 = (bf16[1,80,128]{2,1,0:T(8,128)(2,1)S(1)}, bf16[1,80,128]{2,1,0:T(8,128)(2,1)S(1)}, u32[]{:S(2)}, u32[]{:S(2)}) collective-permute-start(bf16[1,80,128]{2,1,0:T(8,128)(2,1)S(1)} %get-tuple-element.104), channel_id=1, source_target_pairs={{0,2},{1,4},{2,0},{3,6},{4,1},{5,8},{6,3},{7,10},{8,5},{9,12},{10,... | collective-permute-start | bytes 61448 | tf_op jit(solution)/shard_map/ppermute | solution.py:512
  35.8 1.0 %collective-permute-start.8 = (bf16[5,80,128]{2,1,0:T(8,128)(2,1)S(1)}, bf16[5,80,128]{2,1,0:T(8,128)(2,1)S(1)}, u32[]{:S(2)}, u32[]{:S(2)}) collective-permute-start(bf16[5,80,128]{2,1,0:T(8,128)(2,1)S(1)} %get-tuple-element.156.early.refs_5_), channel_id=1, source_target_pairs={{0,2},{1,3},{2,0},{3,1},{4,6},{5,7},{6,4},{7,5},{8,10},{9,11},{10,... | collective-permute-start | bytes 307208 | tf_op jit(solution)/shard_map/ppermute | solution.py:512
  37.4 3.4 %collective-permute-start.7 = (bf16[304,128]{1,0:T(8,128)(2,1)S(1)}, bf16[304,128]{1,0:T(8,128)(2,1)S(1)}, u32[]{:S(2)}, u32[]{:S(2)}) collective-permute-start(bf16[304,128]{1,0:T(8,128)(2,1)S(1)} %dynamic-slice_convert_fusion.1), channel_id=1, source_target_pairs={{0,192},{1,7},{2,194},{3,5},{4,196},{5,3},{6,198},{7,1},{8,200},{9... | collective-permute-start | bytes 233480 | tf_op jit(solution)/shard_map/ppermute | solution.py:559
  40.8 1.8 %collective-permute-done.7 = bf16[304,128]{1,0:T(8,128)(2,1)S(1)} collective-permute-done((bf16[304,128]{1,0:T(8,128)(2,1)S(1)}, bf16[304,128]{1,0:T(8,128)(2,1)S(1)}, u32[]{:S(2)}, u32[]{:S(2)}) %collective-permute-start.7) | collective-permute-done | bytes 77856 | tf_op jit(solution)/shard_map/ppermute | solution.py:559
  42.6 0.9 %collective-permute-start.9 = (bf16[152,128]{1,0:T(8,128)(2,1)S(1)}, bf16[152,128]{1,0:T(8,128)(2,1)S(1)}, u32[]{:S(2)}, u32[]{:S(2)}) collective-permute-start(bf16[152,128]{1,0:T(8,128)(2,1)S(1)} %dynamic-slice_convert_fusion.2), channel_id=1, source_target_pairs={{0,2},{1,65},{2,0},{3,67},{4,6},{5,69},{6,4},{7,71},{8,10},{9,73},... | collective-permute-start | bytes 116744 | tf_op jit(solution)/shard_map/ppermute | solution.py:559
  43.6 2.3 %collective-permute-done.9 = bf16[152,128]{1,0:T(8,128)(2,1)S(1)} collective-permute-done((bf16[152,128]{1,0:T(8,128)(2,1)S(1)}, bf16[152,128]{1,0:T(8,128)(2,1)S(1)}, u32[]{:S(2)}, u32[]{:S(2)}) %collective-permute-start.9) | collective-permute-done | bytes 38944 | tf_op jit(solution)/shard_map/ppermute | solution.py:559
  45.9 2.2 %collective-permute-start.11 = (bf16[152,128]{1,0:T(8,128)(2,1)S(1)}, bf16[152,128]{1,0:T(8,128)(2,1)S(1)}, u32[]{:S(2)}, u32[]{:S(2)}) collective-permute-start(bf16[152,128]{1,0:T(8,128)(2,1)S(1)} %add_convert_fusion.4), channel_id=1, source_target_pairs={{0,6},{1,193},{2,4},{3,195},{4,2},{5,197},{6,0},{7,199},{8,14},{9,... | collective-permute-start | bytes 116744 | tf_op jit(solution)/shard_map/ppermute | solution.py:559
  48.1 3.6 %collective-permute-start.13 = (bf16[11,80,128]{2,1,0:T(8,128)(2,1)S(1)}, bf16[11,80,128]{2,1,0:T(8,128)(2,1)S(1)}, u32[]{:S(2)}, u32[]{:S(2)}) collective-permute-start(bf16[11,80,128]{2,1,0:T(8,128)(2,1)S(1)} %shard_map.181), channel_id=1, source_target_pairs={{0,1},{1,0},{2,3},{3,2},{4,5},{5,4},{6,7},{7,6},{8,9},{9,8},{10,11... | collective-permute-start | bytes 675848 | tf_op jit(solution)/shard_map/ppermute | solution.py:512
  51.7 1.3 %collective-permute-start.12 = (bf16[152,128]{1,0:T(8,128)(2,1)S(1)}, bf16[152,128]{1,0:T(8,128)(2,1)S(1)}, u32[]{:S(2)}, u32[]{:S(2)}) collective-permute-start(bf16[152,128]{1,0:T(8,128)(2,1)S(1)} %add_convert_fusion.3), channel_id=1, source_target_pairs={{0,8},{1,9},{2,10},{3,11},{4,12},{5,13},{6,14},{7,15},{8,0},{9,1},... | collective-permute-start | bytes 116744 | tf_op jit(solution)/shard_map/ppermute | solution.py:559
  53.1 1.6 %collective-permute-done.12 = bf16[152,128]{1,0:T(8,128)(2,1)S(1)} collective-permute-done((bf16[152,128]{1,0:T(8,128)(2,1)S(1)}, bf16[152,128]{1,0:T(8,128)(2,1)S(1)}, u32[]{:S(2)}, u32[]{:S(2)}) %collective-permute-start.12) | collective-permute-done | bytes 38944 | tf_op jit(solution)/shard_map/ppermute | solution.py:559
  54.7 7.8 %collective-permute-start.14 = (bf16[152,128]{1,0:T(8,128)(2,1)S(1)}, bf16[152,128]{1,0:T(8,128)(2,1)S(1)}, u32[]{:S(2)}, u32[]{:S(2)}) collective-permute-start(bf16[152,128]{1,0:T(8,128)(2,1)S(1)} %add_convert_fusion.2), channel_id=1, source_target_pairs={{0,24},{1,25},{2,26},{3,27},{4,28},{5,29},{6,30},{7,31},{8,16},{9,... | collective-permute-start | bytes 116744 | tf_op jit(solution)/shard_map/ppermute | solution.py:559
  62.4 1.9 %shard_map.182 = bf16[1,16,3072]{2,1,0:T(8,128)(2,1)S(1)} custom-call(bf16[4,16,3072]{2,1,0:T(8,128)(2,1)S(1)} %get-tuple-element.122.refs_0_, bf16[4,16,3072]{2,1,0:T(8,128)(2,1)S(1)} %bitcast.16, s32[4,16,16]{2,1,0:T(8,128)S(1)} %copy-done.3, s32[4,8]{1,0:T(4,128)S(1)} %copy-done.6, f32[49,192]{1,0:T(8,128)S(1)} %copy-done.5, ...), custom_call_target="tpu_custom_call" | custom-call | flops 1000000000 | bytes 4000000 | tf_op jit(solution)/shard_map/pallas_call | solution.py:490
  64.4 1.1 %collective-permute-start.15 = (bf16[152,128]{1,0:T(8,128)(2,1)S(1)}, bf16[152,128]{1,0:T(8,128)(2,1)S(1)}, u32[]{:S(2)}, u32[]{:S(2)}) collective-permute-start(bf16[152,128]{1,0:T(8,128)(2,1)S(1)} %add_convert_fusion.1), channel_id=1, source_target_pairs={{0,56},{1,57},{2,58},{3,59},{4,60},{5,61},{6,62},{7,63},{8,48},{9,... | collective-permute-start | bytes 116744 | tf_op jit(solution)/shard_map/ppermute | solution.py:559
  65.5 1.9 %shard_map.183 = bf16[1,16,3072]{2,1,0:T(8,128)(2,1)S(1)} custom-call(bf16[4,16,3072]{2,1,0:T(8,128)(2,1)S(1)} %get-tuple-element.122.refs_0_, bf16[4,16,3072]{2,1,0:T(8,128)(2,1)S(1)} %bitcast.17, s32[4,16,16]{2,1,0:T(8,128)S(1)} %copy-done.3, s32[4,8]{1,0:T(4,128)S(1)} %copy-done.6, f32[49,192]{1,0:T(8,128)S(1)} %copy-done.5, ...), custom_call_target="tpu_custom_call" | custom-call | flops 1000000000 | bytes 4000000 | tf_op jit(solution)/shard_map/pallas_call | solution.py:490
  67.4 1.3 %collective-permute-done.15 = bf16[152,128]{1,0:T(8,128)(2,1)S(1)} collective-permute-done((bf16[152,128]{1,0:T(8,128)(2,1)S(1)}, bf16[152,128]{1,0:T(8,128)(2,1)S(1)}, u32[]{:S(2)}, u32[]{:S(2)}) %collective-permute-start.15) | collective-permute-done | bytes 38944 | tf_op jit(solution)/shard_map/ppermute | solution.py:559
  69.1 1.9 %shard_map.184 = bf16[1,16,3072]{2,1,0:T(8,128)(2,1)S(1)} custom-call(bf16[4,16,3072]{2,1,0:T(8,128)(2,1)S(1)} %get-tuple-element.122.refs_0_, bf16[4,16,3072]{2,1,0:T(8,128)(2,1)S(1)} %bitcast.18, s32[4,16,16]{2,1,0:T(8,128)S(1)} %copy-done.3, s32[4,8]{1,0:T(4,128)S(1)} %copy-done.6, f32[49,192]{1,0:T(8,128)S(1)} %copy-done.5, ...), custom_call_target="tpu_custom_call" | custom-call | flops 1000000000 | bytes 4000000 | tf_op jit(solution)/shard_map/pallas_call | solution.py:490
  71.6 1.7 %collective-permute-start.17 = (bf16[304,128]{1,0:T(8,128)(2,1)S(1)}, bf16[304,128]{1,0:T(8,128)(2,1)S(1)}, u32[]{:S(2)}, u32[]{:S(2)}) collective-permute-start(bf16[304,128]{1,0:T(8,128)(2,1)S(1)} %maximum_select_fusion.3), channel_id=1, source_target_pairs={{0,192},{1,7},{2,194},{3,5},{4,196},{5,3},{6,198},{7,1},{8,200},{9... | collective-permute-start | bytes 233480 | tf_op jit(solution)/shard_map/ppermute | solution.py:559
  73.3 2.1 %shard_map.185 = bf16[1,16,3072]{2,1,0:T(8,128)(2,1)S(1)} custom-call(bf16[4,16,3072]{2,1,0:T(8,128)(2,1)S(1)} %get-tuple-element.122.refs_0_, bf16[4,16,3072]{2,1,0:T(8,128)(2,1)S(1)} %bitcast.19, s32[4,16,16]{2,1,0:T(8,128)S(1)} %copy-done.3, s32[4,8]{1,0:T(4,128)S(1)} %copy-done.6, f32[49,192]{1,0:T(8,128)S(1)} %copy-done.5, ...), custom_call_target="tpu_custom_call" | custom-call | flops 1000000000 | bytes 4000000 | tf_op jit(solution)/shard_map/pallas_call | solution.py:490
  76.3 4.1 %collective-permute-done.18 = bf16[608,128]{1,0:T(8,128)(2,1)S(1)} collective-permute-done((bf16[608,128]{1,0:T(8,128)(2,1)S(1)}, bf16[608,128]{1,0:T(8,128)(2,1)S(1)}, u32[]{:S(2)}, u32[]{:S(2)}) %collective-permute-start.18) | collective-permute-done | bytes 155680 | tf_op jit(solution)/shard_map/ppermute | solution.py:559
  80.5 9.4 %collective-permute-start.19 = (bf16[1216,128]{1,0:T(8,128)(2,1)S(1)}, bf16[1216,128]{1,0:T(8,128)(2,1)S(1)}, u32[]{:S(2)}, u32[]{:S(2)}) collective-permute-start(bf16[1216,128]{1,0:T(8,128)(2,1)S(1)} %maximum_select_fusion.1), channel_id=1, source_target_pairs={{0,1},{1,0},{2,3},{3,2},{4,5},{5,4},{6,7},{7,6},{8,9},{9,8},{10,11... | collective-permute-start | bytes 933896 | tf_op jit(solution)/shard_map/ppermute | solution.py:512
  89.9 0.8 maximum_bitcast_fusion
  91.3 1.1 %shard_map.186 = (f32[49,192]{1,0:T(8,128)}, f32[1,192]{1,0:T(1,128)}, f32[1,192]{1,0:T(1,128)}, f32[192,768]{1,0:T(8,128)}, f32[768]{0:T(1024)}, /*index=5*/f32[192,768]{1,0:T(8,128)}, f32[1,192]{1,0:T(1,128)}) custom-call(bf16[2432,128]{1,0:T(8,128)(2,1)S(1)} %maximum_select_fusion.rows), custom_call_target="tpu_custom_call" | custom-call | flops 1000000 | bytes 4000000 | tf_op jit(solution)/shard_map/pallas_call | solution.py:490
  (61 shorter events, 4.3 us)
Async XLA Ops:
  0.6 1.0 %copy-start = (bf16[1,4,16,3072]{3,2,1,0:T(8,128)(2,1)S(1)}, bf16[1,4,16,3072]{3,2,1,0:T(8,128)(2,1)}, u32[]{:S(2)}) copy-start(bf16[1,4,16,3072]{3,2,1,0:T(8,128)(2,1)} %param.11) | copy-start | bytes 1179652
  2.4 9.2 %copy-start.12 = (f32[768]{0:T(1024)S(1)}, f32[768]{0:T(1024)}, u32[]{:S(2)}) copy-start(f32[768]{0:T(1024)} %param.18) | copy-start | bytes 9220
  2.4 9.2 %copy-start.10 = (bf16[768,192]{0,1:T(8,128)(2,1)S(1)}, bf16[768,192]{0,1:T(8,128)(2,1)}, u32[]{:S(2)}) copy-start(bf16[768,192]{0,1:T(8,128)(2,1)} %param.19) | copy-start | bytes 884740
  2.4 9.2 %copy-start.11 = (bf16[192,768]{1,0:T(8,128)(2,1)S(1)}, bf16[192,768]{1,0:T(8,128)(2,1)}, u32[]{:S(2)}) copy-start(bf16[192,768]{1,0:T(8,128)(2,1)} %param.17) | copy-start | bytes 884740
  2.9 8.5 %collective-permute-start.1 = (bf16[5,80,128]{2,1,0:T(8,128)(2,1)S(1)}, bf16[5,80,128]{2,1,0:T(8,128)(2,1)S(1)}, u32[]{:S(2)}, u32[]{:S(2)}) collective-permute-start(bf16[5,80,128]{2,1,0:T(8,128)(2,1)S(1)} %get-tuple-element.91.early.refs_10_), channel_id=1, source_target_pairs={{0,2},{1,3},{2,0},{3,1},{4,6},{5,7},{6,4},{7,5},{8,10},{9,11},{10,... | collective-permute-start | bytes 307208 | tf_op jit(solution)/shard_map/ppermute | solution.py:512
  5.1 6.3 %collective-permute-start.2 = (bf16[5,80,128]{2,1,0:T(8,128)(2,1)S(1)}, bf16[5,80,128]{2,1,0:T(8,128)(2,1)S(1)}, u32[]{:S(2)}, u32[]{:S(2)}) collective-permute-start(bf16[5,80,128]{2,1,0:T(8,128)(2,1)S(1)} %get-tuple-element.92.late.refs_11_), channel_id=1, source_target_pairs={{0,1},{1,0},{2,4},{3,5},{4,2},{5,3},{6,8},{7,9},{8,6},{9,7},{10,12... | collective-permute-start | bytes 307208 | tf_op jit(solution)/shard_map/ppermute | solution.py:512
  6.3 5.1 %collective-permute-start = (bf16[1,80,128]{2,1,0:T(8,128)(2,1)S(1)}, bf16[1,80,128]{2,1,0:T(8,128)(2,1)S(1)}, u32[]{:S(2)}, u32[]{:S(2)}) collective-permute-start(bf16[1,80,128]{2,1,0:T(8,128)(2,1)S(1)} %get-tuple-element.95), channel_id=1, source_target_pairs={{0,2},{1,4},{2,0},{3,6},{4,1},{5,8},{6,3},{7,10},{8,5},{9,12},{10,... | collective-permute-start | bytes 61448 | tf_op jit(solution)/shard_map/ppermute | solution.py:512
  11.4 1.7 %copy-start.1 = (bf16[1,4,16,3072]{3,2,1,0:T(8,128)(2,1)S(1)}, bf16[1,4,16,3072]{3,2,1,0:T(8,128)(2,1)}, u32[]{:S(2)}) copy-start(bf16[1,4,16,3072]{3,2,1,0:T(8,128)(2,1)} %param.11) | copy-start | bytes 1179652
  11.4 1.7 %copy-start.3 = (s32[4,16,16]{2,1,0:T(8,128)S(1)}, s32[4,16,16]{2,1,0:T(8,128)}, u32[]{:S(2)}) copy-start(s32[4,16,16]{2,1,0:T(8,128)} %refs_2_.9) | copy-start | bytes 12292
  11.4 1.7 %copy-start.4 = (bf16[1,4,16,3072]{3,2,1,0:T(8,128)(2,1)S(1)}, bf16[1,4,16,3072]{3,2,1,0:T(8,128)(2,1)}, u32[]{:S(2)}) copy-start(bf16[1,4,16,3072]{3,2,1,0:T(8,128)(2,1)} %param.21) | copy-start | bytes 1179652
  11.4 1.6 %copy-start.5 = (f32[49,192]{1,0:T(8,128)S(1)}, f32[49,192]{1,0:T(8,128)}, u32[]{:S(2)}) copy-start(f32[49,192]{1,0:T(8,128)} %refs_4_.9) | copy-start | bytes 112900
  11.4 1.6 %copy-start.6 = (s32[4,8]{1,0:T(4,128)S(1)}, s32[4,8]{1,0:T(4,128)}, u32[]{:S(2)}) copy-start(s32[4,8]{1,0:T(4,128)} %refs_3_.9) | copy-start | bytes 388
  11.4 1.6 %copy-start.7 = (f32[192]{0:T(256)S(1)}, f32[192]{0:T(256)}, u32[]{:S(2)}) copy-start(f32[192]{0:T(256)} %param.15) | copy-start | bytes 2308
  11.5 1.6 %copy-start.8 = (f32[192]{0:T(256)S(1)}, f32[192]{0:T(256)}, u32[]{:S(2)}) copy-start(f32[192]{0:T(256)} %param.16) | copy-start | bytes 2308
  11.5 1.6 %copy-start.9 = (f32[192]{0:T(256)S(1)}, f32[192]{0:T(256)}, u32[]{:S(2)}) copy-start(f32[192]{0:T(256)} %param.20) | copy-start | bytes 2308
  11.5 1.6 %collective-permute-start.3 = (bf16[11,80,128]{2,1,0:T(8,128)(2,1)S(1)}, bf16[11,80,128]{2,1,0:T(8,128)(2,1)S(1)}, u32[]{:S(2)}, u32[]{:S(2)}) collective-permute-start(bf16[11,80,128]{2,1,0:T(8,128)(2,1)S(1)} %shard_map.179), channel_id=1, source_target_pairs={{0,1},{1,0},{2,3},{3,2},{4,5},{5,4},{6,7},{7,6},{8,9},{9,8},{10,11... | collective-permute-start | bytes 675848 | tf_op jit(solution)/shard_map/ppermute | solution.py:512
  29.3 1.6 %collective-permute-start.4 = (bf16[1216,128]{1,0:T(8,128)(2,1)S(1)}, bf16[1216,128]{1,0:T(8,128)(2,1)S(1)}, u32[]{:S(2)}, u32[]{:S(2)}) collective-permute-start(bf16[1216,128]{1,0:T(8,128)(2,1)S(1)} %get-tuple-element.101), channel_id=1, source_target_pairs={{0,1},{1,0},{2,3},{3,2},{4,5},{5,4},{6,7},{7,6},{8,9},{9,8},{10,11... | collective-permute-start | bytes 933896 | tf_op jit(solution)/shard_map/ppermute | solution.py:512
  31.0 6.4 %collective-permute-start.5 = (bf16[608,128]{1,0:T(8,128)(2,1)S(1)}, bf16[608,128]{1,0:T(8,128)(2,1)S(1)}, u32[]{:S(2)}, u32[]{:S(2)}) collective-permute-start(bf16[608,128]{1,0:T(8,128)(2,1)S(1)} %dynamic-slice_convert_fusion), channel_id=1, source_target_pairs={{0,64},{1,3},{2,66},{3,1},{4,68},{5,7},{6,70},{7,5},{8,72},{9,11},... | collective-permute-start | bytes 466952 | tf_op jit(solution)/shard_map/ppermute | solution.py:559
  32.0 5.4 %collective-permute-start.6 = (bf16[1,80,128]{2,1,0:T(8,128)(2,1)S(1)}, bf16[1,80,128]{2,1,0:T(8,128)(2,1)S(1)}, u32[]{:S(2)}, u32[]{:S(2)}) collective-permute-start(bf16[1,80,128]{2,1,0:T(8,128)(2,1)S(1)} %get-tuple-element.104), channel_id=1, source_target_pairs={{0,2},{1,4},{2,0},{3,6},{4,1},{5,8},{6,3},{7,10},{8,5},{9,12},{10,... | collective-permute-start | bytes 61448 | tf_op jit(solution)/shard_map/ppermute | solution.py:512
  35.8 5.0 %collective-permute-start.8 = (bf16[5,80,128]{2,1,0:T(8,128)(2,1)S(1)}, bf16[5,80,128]{2,1,0:T(8,128)(2,1)S(1)}, u32[]{:S(2)}, u32[]{:S(2)}) collective-permute-start(bf16[5,80,128]{2,1,0:T(8,128)(2,1)S(1)} %get-tuple-element.156.early.refs_5_), channel_id=1, source_target_pairs={{0,2},{1,3},{2,0},{3,1},{4,6},{5,7},{6,4},{7,5},{8,10},{9,11},{10,... | collective-permute-start | bytes 307208 | tf_op jit(solution)/shard_map/ppermute | solution.py:512
  37.4 5.2 %collective-permute-start.7 = (bf16[304,128]{1,0:T(8,128)(2,1)S(1)}, bf16[304,128]{1,0:T(8,128)(2,1)S(1)}, u32[]{:S(2)}, u32[]{:S(2)}) collective-permute-start(bf16[304,128]{1,0:T(8,128)(2,1)S(1)} %dynamic-slice_convert_fusion.1), channel_id=1, source_target_pairs={{0,192},{1,7},{2,194},{3,5},{4,196},{5,3},{6,198},{7,1},{8,200},{9... | collective-permute-start | bytes 233480 | tf_op jit(solution)/shard_map/ppermute | solution.py:559
  40.8 2.8 %collective-permute-start.10 = (bf16[5,80,128]{2,1,0:T(8,128)(2,1)S(1)}, bf16[5,80,128]{2,1,0:T(8,128)(2,1)S(1)}, u32[]{:S(2)}, u32[]{:S(2)}) collective-permute-start(bf16[5,80,128]{2,1,0:T(8,128)(2,1)S(1)} %get-tuple-element.157.late.refs_6_), channel_id=1, source_target_pairs={{0,1},{1,0},{2,4},{3,5},{4,2},{5,3},{6,8},{7,9},{8,6},{9,7},{10,12... | collective-permute-start | bytes 307208 | tf_op jit(solution)/shard_map/ppermute | solution.py:512
  42.6 3.2 %collective-permute-start.9 = (bf16[152,128]{1,0:T(8,128)(2,1)S(1)}, bf16[152,128]{1,0:T(8,128)(2,1)S(1)}, u32[]{:S(2)}, u32[]{:S(2)}) collective-permute-start(bf16[152,128]{1,0:T(8,128)(2,1)S(1)} %dynamic-slice_convert_fusion.2), channel_id=1, source_target_pairs={{0,2},{1,65},{2,0},{3,67},{4,6},{5,69},{6,4},{7,71},{8,10},{9,73},... | collective-permute-start | bytes 116744 | tf_op jit(solution)/shard_map/ppermute | solution.py:559
  45.9 5.8 %collective-permute-start.11 = (bf16[152,128]{1,0:T(8,128)(2,1)S(1)}, bf16[152,128]{1,0:T(8,128)(2,1)S(1)}, u32[]{:S(2)}, u32[]{:S(2)}) collective-permute-start(bf16[152,128]{1,0:T(8,128)(2,1)S(1)} %add_convert_fusion.4), channel_id=1, source_target_pairs={{0,6},{1,193},{2,4},{3,195},{4,2},{5,197},{6,0},{7,199},{8,14},{9,... | collective-permute-start | bytes 116744 | tf_op jit(solution)/shard_map/ppermute | solution.py:559
  48.1 6.6 %collective-permute-start.13 = (bf16[11,80,128]{2,1,0:T(8,128)(2,1)S(1)}, bf16[11,80,128]{2,1,0:T(8,128)(2,1)S(1)}, u32[]{:S(2)}, u32[]{:S(2)}) collective-permute-start(bf16[11,80,128]{2,1,0:T(8,128)(2,1)S(1)} %shard_map.181), channel_id=1, source_target_pairs={{0,1},{1,0},{2,3},{3,2},{4,5},{5,4},{6,7},{7,6},{8,9},{9,8},{10,11... | collective-permute-start | bytes 675848 | tf_op jit(solution)/shard_map/ppermute | solution.py:512
  51.7 2.9 %collective-permute-start.12 = (bf16[152,128]{1,0:T(8,128)(2,1)S(1)}, bf16[152,128]{1,0:T(8,128)(2,1)S(1)}, u32[]{:S(2)}, u32[]{:S(2)}) collective-permute-start(bf16[152,128]{1,0:T(8,128)(2,1)S(1)} %add_convert_fusion.3), channel_id=1, source_target_pairs={{0,8},{1,9},{2,10},{3,11},{4,12},{5,13},{6,14},{7,15},{8,0},{9,1},... | collective-permute-start | bytes 116744 | tf_op jit(solution)/shard_map/ppermute | solution.py:559
  54.7 9.7 %collective-permute-start.14 = (bf16[152,128]{1,0:T(8,128)(2,1)S(1)}, bf16[152,128]{1,0:T(8,128)(2,1)S(1)}, u32[]{:S(2)}, u32[]{:S(2)}) collective-permute-start(bf16[152,128]{1,0:T(8,128)(2,1)S(1)} %add_convert_fusion.2), channel_id=1, source_target_pairs={{0,24},{1,25},{2,26},{3,27},{4,28},{5,29},{6,30},{7,31},{8,16},{9,... | collective-permute-start | bytes 116744 | tf_op jit(solution)/shard_map/ppermute | solution.py:559
  64.4 4.3 %collective-permute-start.15 = (bf16[152,128]{1,0:T(8,128)(2,1)S(1)}, bf16[152,128]{1,0:T(8,128)(2,1)S(1)}, u32[]{:S(2)}, u32[]{:S(2)}) collective-permute-start(bf16[152,128]{1,0:T(8,128)(2,1)S(1)} %add_convert_fusion.1), channel_id=1, source_target_pairs={{0,56},{1,57},{2,58},{3,59},{4,60},{5,61},{6,62},{7,63},{8,48},{9,... | collective-permute-start | bytes 116744 | tf_op jit(solution)/shard_map/ppermute | solution.py:559
  68.7 2.9 %collective-permute-start.16 = (bf16[152,128]{1,0:T(8,128)(2,1)S(1)}, bf16[152,128]{1,0:T(8,128)(2,1)S(1)}, u32[]{:S(2)}, u32[]{:S(2)}) collective-permute-start(bf16[152,128]{1,0:T(8,128)(2,1)S(1)} %add_convert_fusion), channel_id=1, source_target_pairs={{0,2},{1,65},{2,0},{3,67},{4,6},{5,69},{6,4},{7,71},{8,10},{9,73},... | collective-permute-start | bytes 116744 | tf_op jit(solution)/shard_map/ppermute | solution.py:559
  71.6 4.5 %collective-permute-start.17 = (bf16[304,128]{1,0:T(8,128)(2,1)S(1)}, bf16[304,128]{1,0:T(8,128)(2,1)S(1)}, u32[]{:S(2)}, u32[]{:S(2)}) collective-permute-start(bf16[304,128]{1,0:T(8,128)(2,1)S(1)} %maximum_select_fusion.3), channel_id=1, source_target_pairs={{0,192},{1,7},{2,194},{3,5},{4,196},{5,3},{6,198},{7,1},{8,200},{9... | collective-permute-start | bytes 233480 | tf_op jit(solution)/shard_map/ppermute | solution.py:559
  76.2 4.2 %collective-permute-start.18 = (bf16[608,128]{1,0:T(8,128)(2,1)S(1)}, bf16[608,128]{1,0:T(8,128)(2,1)S(1)}, u32[]{:S(2)}, u32[]{:S(2)}) collective-permute-start(bf16[608,128]{1,0:T(8,128)(2,1)S(1)} %maximum_select_fusion.2), channel_id=1, source_target_pairs={{0,64},{1,3},{2,66},{3,1},{4,68},{5,7},{6,70},{7,5},{8,72},{9,11},... | collective-permute-start | bytes 466952 | tf_op jit(solution)/shard_map/ppermute | solution.py:559
  80.5 10.6 %collective-permute-start.19 = (bf16[1216,128]{1,0:T(8,128)(2,1)S(1)}, bf16[1216,128]{1,0:T(8,128)(2,1)S(1)}, u32[]{:S(2)}, u32[]{:S(2)}) collective-permute-start(bf16[1216,128]{1,0:T(8,128)(2,1)S(1)} %maximum_select_fusion.1), channel_id=1, source_target_pairs={{0,1},{1,0},{2,3},{3,2},{4,5},{5,4},{6,7},{7,6},{8,9},{9,8},{10,11... | collective-permute-start | bytes 933896 | tf_op jit(solution)/shard_map/ppermute | solution.py:512
  (1 other events, 0.8 us)

commit v3 on v2

--- a/solution.py
+++ b/solution.py
@@ -20,7 +20,11 @@
 STRIP = 80
 CELLS = TILE * TILE
 INV_SQRT2 = 0.7071067811865476
-INV_SQRT_2PI = 0.3989422804014327
+LOG_SQRT_2PI = 0.5 * math.log(2.0 * math.pi)
+TAIL = [
+    0.5 * math.sqrt(2.0 * math.pi) * c
+    for c in (0.254829592, -0.284496736, 1.421413741, -1.453152027, 1.061405429)
+]
 EXTRA = 128
 HALF_ROWS = 6 * C + EXTRA // 2
 F32 = jnp.float32
@@ -213,7 +217,7 @@
             turned = following
         return carry
 
-    lax.fori_loop(0, len(tiles), one_tile, 0)
+    lax.fori_loop(0, len(tiles), one_tile, 0, unroll=True)
 
 
 def spread_taps(dw_ref, wide, taps):
@@ -256,7 +260,7 @@
                     out[s, 3 * q + m, 8 * h : 8 * h + 8, :] = total[q]
             return carry
 
-        lax.fori_loop(0, count, body, 0)
+        lax.fori_loop(0, count, body, 0, unroll=min(2, count))
 
 
 def kernel_grad(padded, shifted, back, wide):
@@ -275,7 +279,7 @@
                 return tuple(totals)
 
             start = tuple(jnp.zeros((8, 128), F32) for _ in range(KS))
-            totals = lax.fori_loop(0, TPD, body, start)
+            totals = lax.fori_loop(0, TPD, body, start, unroll=2)
             for j in range(KS):
                 k = KS * i + j
                 wide[m, k : k + 1, :] = jnp.sum(totals[j], axis=0, keepdims=True)
@@ -364,19 +368,16 @@
         shifted = (normed * gain + bias_ref[...]).astype(BF16)
         norm_rows[s] = shifted
         preact = jnp.dot(shifted, w_in[...], preferred_element_type=F32) + b_in[...]
-        bell = jnp.exp(-0.5 * preact * preact)
+        bell = jnp.exp(-0.5 * preact * preact - LOG_SQRT_2PI)
         below = 1.0 + (0.3275911 * INV_SQRT2) * jnp.abs(preact)
         u = pl.reciprocal(below, approx=True)
         u = u * (2.0 - below * u)
-        series = u * (
-            0.5 * 0.254829592
-            + u * (0.5 * -0.284496736 + u * (0.5 * 1.421413741 + u * (0.5 * -1.453152027 + u * (0.5 * 1.061405429))))
-        )
+        series = u * (TAIL[0] + u * (TAIL[1] + u * (TAIL[2] + u * (TAIL[3] + u * TAIL[4]))))
         tail = series * bell
         cdf = jnp.where(preact >= 0.0, 1.0 - tail, tail)
         hidden = (preact * cdf).astype(BF16)
         hid_rows[s] = hidden
-        slope = cdf + preact * bell * INV_SQRT_2PI
+        slope = cdf + preact * bell
         branch = dot_last(hidden, w_out[...])
         rows_a[:, 0:C] = branch * scale
 

time: 92.5 us -> 92.1 us (level)
  no operation moved by 1% of the time
where the time goes in v3:
time: 92.1 us; the launch traced here: 92 us
  starting transfers between devices  45.1 us (49%)
  Pallas kernels  24.7 us (27%)
  waiting for transfers between devices  18 us (20%)
  local copies, waits for them, and re-layouts  1.87 us (2%)
  other arithmetic  1.35 us (1%)
  between operations  0.97 us (1%)
    ppermute x10, starting transfers between devices, swap(): lax.ppermute(block, axis, [(i, partner(i)) for i in range(lax.axis_size(a...  25 us
    pallas_call x9, Pallas kernels, call(): pl.pallas_call(kernel, out_shape=out_shape, in_specs=[whole(pltpu.SMEM if...  24.7 us
    ppermute x10, starting transfers between devices, trade(): return lax.ppermute(block, ('dp', 'tiles'), route)  20.1 us
    ppermute x10, waiting for transfers between devices, trade(): return lax.ppermute(block, ('dp', 'tiles'), route)  12.6 us
    ppermute x10, waiting for transfers between devices, swap(): lax.ppermute(block, axis, [(i, partner(i)) for i in range(lax.axis_size(a...  5.4 us
  transfers between devices with their start and end apart: 20, of which 12 were waited for; matrix products, arithmetic and copies ran while one was open for 1% of the time, Pallas kernels for 8%

profile of v3, /device:TPU:1, one launch (start us, length us, event | category | flops | bytes accessed | tf_op | source)
XLA Modules:
  0.0 92.0 jit_solution(4528027577276412373)
XLA Ops:
  0.7 1.0 %copy-done = bf16[1,4,16,3072]{3,2,1,0:T(8,128)(2,1)S(1)} copy-done((bf16[1,4,16,3072]{3,2,1,0:T(8,128)(2,1)S(1)}, bf16[1,4,16,3072]{3,2,1,0:T(8,128)(2,1)}, u32[]{:S(2)}) %copy-start) | copy-done | bytes 393240
  2.9 2.2 %collective-permute-start.1 = (bf16[5,80,128]{2,1,0:T(8,128)(2,1)S(1)}, bf16[5,80,128]{2,1,0:T(8,128)(2,1)S(1)}, u32[]{:S(2)}, u32[]{:S(2)}) collective-permute-start(bf16[5,80,128]{2,1,0:T(8,128)(2,1)S(1)} %get-tuple-element.91.early.refs_10_), channel_id=1, source_target_pairs={{0,2},{1,3},{2,0},{3,1},{4,6},{5,7},{6,4},{7,5},{8,10},{9,11},{10,... | collective-permute-start | bytes 307208 | tf_op jit(solution)/shard_map/ppermute | solution.py:513
  5.1 1.2 %collective-permute-start.2 = (bf16[5,80,128]{2,1,0:T(8,128)(2,1)S(1)}, bf16[5,80,128]{2,1,0:T(8,128)(2,1)S(1)}, u32[]{:S(2)}, u32[]{:S(2)}) collective-permute-start(bf16[5,80,128]{2,1,0:T(8,128)(2,1)S(1)} %get-tuple-element.92.late.refs_11_), channel_id=1, source_target_pairs={{0,1},{1,0},{2,4},{3,5},{4,2},{5,3},{6,8},{7,9},{8,6},{9,7},{10,12... | collective-permute-start | bytes 307208 | tf_op jit(solution)/shard_map/ppermute | solution.py:513
  6.3 3.6 %collective-permute-start = (bf16[1,80,128]{2,1,0:T(8,128)(2,1)S(1)}, bf16[1,80,128]{2,1,0:T(8,128)(2,1)S(1)}, u32[]{:S(2)}, u32[]{:S(2)}) collective-permute-start(bf16[1,80,128]{2,1,0:T(8,128)(2,1)S(1)} %get-tuple-element.95), channel_id=1, source_target_pairs={{0,2},{1,4},{2,0},{3,6},{4,1},{5,8},{6,3},{7,10},{8,5},{9,12},{10,... | collective-permute-start | bytes 61448 | tf_op jit(solution)/shard_map/ppermute | solution.py:513
  9.9 1.5 %collective-permute-done.refs_16_ = bf16[1,80,128]{2,1,0:T(8,128)(2,1)S(1)} collective-permute-done((bf16[1,80,128]{2,1,0:T(8,128)(2,1)S(1)}, bf16[1,80,128]{2,1,0:T(8,128)(2,1)S(1)}, u32[]{:S(2)}, u32[]{:S(2)}) %collective-permute-start) | collective-permute-done | bytes 20512 | tf_op jit(solution)/shard_map/ppermute | solution.py:513
  11.7 1.4 %collective-permute-done.3.refs_17_ = bf16[11,80,128]{2,1,0:T(8,128)(2,1)S(1)} collective-permute-done((bf16[11,80,128]{2,1,0:T(8,128)(2,1)S(1)}, bf16[11,80,128]{2,1,0:T(8,128)(2,1)S(1)}, u32[]{:S(2)}, u32[]{:S(2)}) %collective-permute-start.3) | collective-permute-done | bytes 225312 | tf_op jit(solution)/shard_map/ppermute | solution.py:513
  13.1 15.5 %shard_map.180 = (bf16[4,16,3072]{2,1,0:T(8,128)(2,1)}, bf16[4,16,3072]{2,1,0:T(8,128)(2,1)S(1)}, f32[1216,128]{1,0:T(8,128)S(1)}, bf16[1216,128]{1,0:T(8,128)(2...) custom-call(bf16[4,16,3072]{2,1,0:T(8,128)(2,1)S(1)} %bitcast.14, ...), custom_call_target="tpu_custom_call" | custom-call | flops 2000000000 | bytes 4000000 | tf_op jit(solution)/shard_map/pallas_call | solution.py:491
  28.8 1.5 %collective-permute-done.4 = bf16[1216,128]{1,0:T(8,128)(2,1)S(1)} collective-permute-done((bf16[1216,128]{1,0:T(8,128)(2,1)S(1)}, bf16[1216,128]{1,0:T(8,128)(2,1)S(1)}, u32[]{:S(2)}, u32[]{:S(2)}) %collective-permute-start.4) | collective-permute-done | bytes 311328 | tf_op jit(solution)/shard_map/ppermute | solution.py:513
  30.4 1.0 %collective-permute-start.5 = (bf16[608,128]{1,0:T(8,128)(2,1)S(1)}, bf16[608,128]{1,0:T(8,128)(2,1)S(1)}, u32[]{:S(2)}, u32[]{:S(2)}) collective-permute-start(bf16[608,128]{1,0:T(8,128)(2,1)S(1)} %dynamic-slice_convert_fusion), channel_id=1, source_target_pairs={{0,64},{1,3},{2,66},{3,1},{4,68},{5,7},{6,70},{7,5},{8,72},{9,11},... | collective-permute-start | bytes 466952 | tf_op jit(solution)/shard_map/ppermute | solution.py:560
  31.4 3.8 %collective-permute-start.6 = (bf16[1,80,128]{2,1,0:T(8,128)(2,1)S(1)}, bf16[1,80,128]{2,1,0:T(8,128)(2,1)S(1)}, u32[]{:S(2)}, u32[]{:S(2)}) collective-permute-start(bf16[1,80,128]{2,1,0:T(8,128)(2,1)S(1)} %get-tuple-element.104), channel_id=1, source_target_pairs={{0,2},{1,4},{2,0},{3,6},{4,1},{5,8},{6,3},{7,10},{8,5},{9,12},{10,... | collective-permute-start | bytes 61448 | tf_op jit(solution)/shard_map/ppermute | solution.py:513
  35.1 1.0 %collective-permute-start.8 = (bf16[5,80,128]{2,1,0:T(8,128)(2,1)S(1)}, bf16[5,80,128]{2,1,0:T(8,128)(2,1)S(1)}, u32[]{:S(2)}, u32[]{:S(2)}) collective-permute-start(bf16[5,80,128]{2,1,0:T(8,128)(2,1)S(1)} %get-tuple-element.156.early.refs_5_), channel_id=1, source_target_pairs={{0,2},{1,3},{2,0},{3,1},{4,6},{5,7},{6,4},{7,5},{8,10},{9,11},{10,... | collective-permute-start | bytes 307208 | tf_op jit(solution)/shard_map/ppermute | solution.py:513
  36.8 3.4 %collective-permute-start.7 = (bf16[304,128]{1,0:T(8,128)(2,1)S(1)}, bf16[304,128]{1,0:T(8,128)(2,1)S(1)}, u32[]{:S(2)}, u32[]{:S(2)}) collective-permute-start(bf16[304,128]{1,0:T(8,128)(2,1)S(1)} %dynamic-slice_convert_fusion.1), channel_id=1, source_target_pairs={{0,192},{1,7},{2,194},{3,5},{4,196},{5,3},{6,198},{7,1},{8,200},{9... | collective-permute-start | bytes 233480 | tf_op jit(solution)/shard_map/ppermute | solution.py:560
  40.2 1.8 %collective-permute-done.7 = bf16[304,128]{1,0:T(8,128)(2,1)S(1)} collective-permute-done((bf16[304,128]{1,0:T(8,128)(2,1)S(1)}, bf16[304,128]{1,0:T(8,128)(2,1)S(1)}, u32[]{:S(2)}, u32[]{:S(2)}) %collective-permute-start.7) | collective-permute-done | bytes 77856 | tf_op jit(solution)/shard_map/ppermute | solution.py:560
  42.0 0.9 %collective-permute-start.9 = (bf16[152,128]{1,0:T(8,128)(2,1)S(1)}, bf16[152,128]{1,0:T(8,128)(2,1)S(1)}, u32[]{:S(2)}, u32[]{:S(2)}) collective-permute-start(bf16[152,128]{1,0:T(8,128)(2,1)S(1)} %dynamic-slice_convert_fusion.2), channel_id=1, source_target_pairs={{0,2},{1,65},{2,0},{3,67},{4,6},{5,69},{6,4},{7,71},{8,10},{9,73},... | collective-permute-start | bytes 116744 | tf_op jit(solution)/shard_map/ppermute | solution.py:560
  42.9 2.3 %collective-permute-done.9 = bf16[152,128]{1,0:T(8,128)(2,1)S(1)} collective-permute-done((bf16[152,128]{1,0:T(8,128)(2,1)S(1)}, bf16[152,128]{1,0:T(8,128)(2,1)S(1)}, u32[]{:S(2)}, u32[]{:S(2)}) %collective-permute-start.9) | collective-permute-done | bytes 38944 | tf_op jit(solution)/shard_map/ppermute | solution.py:560
  45.3 2.2 %collective-permute-start.11 = (bf16[152,128]{1,0:T(8,128)(2,1)S(1)}, bf16[152,128]{1,0:T(8,128)(2,1)S(1)}, u32[]{:S(2)}, u32[]{:S(2)}) collective-permute-start(bf16[152,128]{1,0:T(8,128)(2,1)S(1)} %add_convert_fusion.4), channel_id=1, source_target_pairs={{0,6},{1,193},{2,4},{3,195},{4,2},{5,197},{6,0},{7,199},{8,14},{9,... | collective-permute-start | bytes 116744 | tf_op jit(solution)/shard_map/ppermute | solution.py:560
  47.5 3.6 %collective-permute-start.13 = (bf16[11,80,128]{2,1,0:T(8,128)(2,1)S(1)}, bf16[11,80,128]{2,1,0:T(8,128)(2,1)S(1)}, u32[]{:S(2)}, u32[]{:S(2)}) collective-permute-start(bf16[11,80,128]{2,1,0:T(8,128)(2,1)S(1)} %shard_map.181), channel_id=1, source_target_pairs={{0,1},{1,0},{2,3},{3,2},{4,5},{5,4},{6,7},{7,6},{8,9},{9,8},{10,11... | collective-permute-start | bytes 675848 | tf_op jit(solution)/shard_map/ppermute | solution.py:513
  51.1 1.3 %collective-permute-start.12 = (bf16[152,128]{1,0:T(8,128)(2,1)S(1)}, bf16[152,128]{1,0:T(8,128)(2,1)S(1)}, u32[]{:S(2)}, u32[]{:S(2)}) collective-permute-start(bf16[152,128]{1,0:T(8,128)(2,1)S(1)} %add_convert_fusion.3), channel_id=1, source_target_pairs={{0,8},{1,9},{2,10},{3,11},{4,12},{5,13},{6,14},{7,15},{8,0},{9,1},... | collective-permute-start | bytes 116744 | tf_op jit(solution)/shard_map/ppermute | solution.py:560
  52.4 1.6 %collective-permute-done.12 = bf16[152,128]{1,0:T(8,128)(2,1)S(1)} collective-permute-done((bf16[152,128]{1,0:T(8,128)(2,1)S(1)}, bf16[152,128]{1,0:T(8,128)(2,1)S(1)}, u32[]{:S(2)}, u32[]{:S(2)}) %collective-permute-start.12) | collective-permute-done | bytes 38944 | tf_op jit(solution)/shard_map/ppermute | solution.py:560
  54.0 7.8 %collective-permute-start.14 = (bf16[152,128]{1,0:T(8,128)(2,1)S(1)}, bf16[152,128]{1,0:T(8,128)(2,1)S(1)}, u32[]{:S(2)}, u32[]{:S(2)}) collective-permute-start(bf16[152,128]{1,0:T(8,128)(2,1)S(1)} %add_convert_fusion.2), channel_id=1, source_target_pairs={{0,24},{1,25},{2,26},{3,27},{4,28},{5,29},{6,30},{7,31},{8,16},{9,... | collective-permute-start | bytes 116744 | tf_op jit(solution)/shard_map/ppermute | solution.py:560
  61.8 1.9 %shard_map.182 = bf16[1,16,3072]{2,1,0:T(8,128)(2,1)S(1)} custom-call(bf16[4,16,3072]{2,1,0:T(8,128)(2,1)S(1)} %get-tuple-element.122.refs_0_, bf16[4,16,3072]{2,1,0:T(8,128)(2,1)S(1)} %bitcast.16, s32[4,16,16]{2,1,0:T(8,128)S(1)} %copy-done.3, s32[4,8]{1,0:T(4,128)S(1)} %copy-done.6, f32[49,192]{1,0:T(8,128)S(1)} %copy-done.5, ...), custom_call_target="tpu_custom_call" | custom-call | flops 1000000000 | bytes 4000000 | tf_op jit(solution)/shard_map/pallas_call | solution.py:491
  63.8 1.1 %collective-permute-start.15 = (bf16[152,128]{1,0:T(8,128)(2,1)S(1)}, bf16[152,128]{1,0:T(8,128)(2,1)S(1)}, u32[]{:S(2)}, u32[]{:S(2)}) collective-permute-start(bf16[152,128]{1,0:T(8,128)(2,1)S(1)} %add_convert_fusion.1), channel_id=1, source_target_pairs={{0,56},{1,57},{2,58},{3,59},{4,60},{5,61},{6,62},{7,63},{8,48},{9,... | collective-permute-start | bytes 116744 | tf_op jit(solution)/shard_map/ppermute | solution.py:560
  64.9 1.9 %shard_map.183 = bf16[1,16,3072]{2,1,0:T(8,128)(2,1)S(1)} custom-call(bf16[4,16,3072]{2,1,0:T(8,128)(2,1)S(1)} %get-tuple-element.122.refs_0_, bf16[4,16,3072]{2,1,0:T(8,128)(2,1)S(1)} %bitcast.17, s32[4,16,16]{2,1,0:T(8,128)S(1)} %copy-done.3, s32[4,8]{1,0:T(4,128)S(1)} %copy-done.6, f32[49,192]{1,0:T(8,128)S(1)} %copy-done.5, ...), custom_call_target="tpu_custom_call" | custom-call | flops 1000000000 | bytes 4000000 | tf_op jit(solution)/shard_map/pallas_call | solution.py:491
  66.8 1.3 %collective-permute-done.15 = bf16[152,128]{1,0:T(8,128)(2,1)S(1)} collective-permute-done((bf16[152,128]{1,0:T(8,128)(2,1)S(1)}, bf16[152,128]{1,0:T(8,128)(2,1)S(1)}, u32[]{:S(2)}, u32[]{:S(2)}) %collective-permute-start.15) | collective-permute-done | bytes 38944 | tf_op jit(solution)/shard_map/ppermute | solution.py:560
  68.7 1.9 %shard_map.184 = bf16[1,16,3072]{2,1,0:T(8,128)(2,1)S(1)} custom-call(bf16[4,16,3072]{2,1,0:T(8,128)(2,1)S(1)} %get-tuple-element.122.refs_0_, bf16[4,16,3072]{2,1,0:T(8,128)(2,1)S(1)} %bitcast.18, s32[4,16,16]{2,1,0:T(8,128)S(1)} %copy-done.3, s32[4,8]{1,0:T(4,128)S(1)} %copy-done.6, f32[49,192]{1,0:T(8,128)S(1)} %copy-done.5, ...), custom_call_target="tpu_custom_call" | custom-call | flops 1000000000 | bytes 4000000 | tf_op jit(solution)/shard_map/pallas_call | solution.py:491
  71.2 1.7 %collective-permute-start.17 = (bf16[304,128]{1,0:T(8,128)(2,1)S(1)}, bf16[304,128]{1,0:T(8,128)(2,1)S(1)}, u32[]{:S(2)}, u32[]{:S(2)}) collective-permute-start(bf16[304,128]{1,0:T(8,128)(2,1)S(1)} %maximum_select_fusion.3), channel_id=1, source_target_pairs={{0,192},{1,7},{2,194},{3,5},{4,196},{5,3},{6,198},{7,1},{8,200},{9... | collective-permute-start | bytes 233480 | tf_op jit(solution)/shard_map/ppermute | solution.py:560
  72.9 1.9 %shard_map.185 = bf16[1,16,3072]{2,1,0:T(8,128)(2,1)S(1)} custom-call(bf16[4,16,3072]{2,1,0:T(8,128)(2,1)S(1)} %get-tuple-element.122.refs_0_, bf16[4,16,3072]{2,1,0:T(8,128)(2,1)S(1)} %bitcast.19, s32[4,16,16]{2,1,0:T(8,128)S(1)} %copy-done.3, s32[4,8]{1,0:T(4,128)S(1)} %copy-done.6, f32[49,192]{1,0:T(8,128)S(1)} %copy-done.5, ...), custom_call_target="tpu_custom_call" | custom-call | flops 1000000000 | bytes 4000000 | tf_op jit(solution)/shard_map/pallas_call | solution.py:491
  74.8 0.9 %collective-permute-done.17 = bf16[304,128]{1,0:T(8,128)(2,1)S(1)} collective-permute-done((bf16[304,128]{1,0:T(8,128)(2,1)S(1)}, bf16[304,128]{1,0:T(8,128)(2,1)S(1)}, u32[]{:S(2)}, u32[]{:S(2)}) %collective-permute-start.17) | collective-permute-done | bytes 77856 | tf_op jit(solution)/shard_map/ppermute | solution.py:560
  75.9 4.1 %collective-permute-done.18 = bf16[608,128]{1,0:T(8,128)(2,1)S(1)} collective-permute-done((bf16[608,128]{1,0:T(8,128)(2,1)S(1)}, bf16[608,128]{1,0:T(8,128)(2,1)S(1)}, u32[]{:S(2)}, u32[]{:S(2)}) %collective-permute-start.18) | collective-permute-done | bytes 155680 | tf_op jit(solution)/shard_map/ppermute | solution.py:560
  80.1 9.4 %collective-permute-start.19 = (bf16[1216,128]{1,0:T(8,128)(2,1)S(1)}, bf16[1216,128]{1,0:T(8,128)(2,1)S(1)}, u32[]{:S(2)}, u32[]{:S(2)}) collective-permute-start(bf16[1216,128]{1,0:T(8,128)(2,1)S(1)} %maximum_select_fusion.1), channel_id=1, source_target_pairs={{0,1},{1,0},{2,3},{3,2},{4,5},{5,4},{6,7},{7,6},{8,9},{9,8},{10,11... | collective-permute-start | bytes 933896 | tf_op jit(solution)/shard_map/ppermute | solution.py:513
  89.5 0.8 maximum_bitcast_fusion
  90.9 1.1 %shard_map.186 = (f32[49,192]{1,0:T(8,128)}, f32[1,192]{1,0:T(1,128)}, f32[1,192]{1,0:T(1,128)}, f32[192,768]{1,0:T(8,128)}, f32[768]{0:T(1024)}, /*index=5*/f32[192,768]{1,0:T(8,128)}, f32[1,192]{1,0:T(1,128)}) custom-call(bf16[2432,128]{1,0:T(8,128)(2,1)S(1)} %maximum_select_fusion.rows), custom_call_target="tpu_custom_call" | custom-call | flops 1000000 | bytes 4000000 | tf_op jit(solution)/shard_map/pallas_call | solution.py:491
  (61 shorter events, 4.6 us)
Async XLA Ops:
  0.6 1.0 %copy-start = (bf16[1,4,16,3072]{3,2,1,0:T(8,128)(2,1)S(1)}, bf16[1,4,16,3072]{3,2,1,0:T(8,128)(2,1)}, u32[]{:S(2)}) copy-start(bf16[1,4,16,3072]{3,2,1,0:T(8,128)(2,1)} %param.11) | copy-start | bytes 1179652
  2.4 9.2 %copy-start.12 = (f32[768]{0:T(1024)S(1)}, f32[768]{0:T(1024)}, u32[]{:S(2)}) copy-start(f32[768]{0:T(1024)} %param.18) | copy-start | bytes 9220
  2.4 9.2 %copy-start.10 = (bf16[768,192]{0,1:T(8,128)(2,1)S(1)}, bf16[768,192]{0,1:T(8,128)(2,1)}, u32[]{:S(2)}) copy-start(bf16[768,192]{0,1:T(8,128)(2,1)} %param.19) | copy-start | bytes 884740
  2.4 9.2 %copy-start.11 = (bf16[192,768]{1,0:T(8,128)(2,1)S(1)}, bf16[192,768]{1,0:T(8,128)(2,1)}, u32[]{:S(2)}) copy-start(bf16[192,768]{1,0:T(8,128)(2,1)} %param.17) | copy-start | bytes 884740
  2.9 8.5 %collective-permute-start.1 = (bf16[5,80,128]{2,1,0:T(8,128)(2,1)S(1)}, bf16[5,80,128]{2,1,0:T(8,128)(2,1)S(1)}, u32[]{:S(2)}, u32[]{:S(2)}) collective-permute-start(bf16[5,80,128]{2,1,0:T(8,128)(2,1)S(1)} %get-tuple-element.91.early.refs_10_), channel_id=1, source_target_pairs={{0,2},{1,3},{2,0},{3,1},{4,6},{5,7},{6,4},{7,5},{8,10},{9,11},{10,... | collective-permute-start | bytes 307208 | tf_op jit(solution)/shard_map/ppermute | solution.py:513
  5.1 6.3 %collective-permute-start.2 = (bf16[5,80,128]{2,1,0:T(8,128)(2,1)S(1)}, bf16[5,80,128]{2,1,0:T(8,128)(2,1)S(1)}, u32[]{:S(2)}, u32[]{:S(2)}) collective-permute-start(bf16[5,80,128]{2,1,0:T(8,128)(2,1)S(1)} %get-tuple-element.92.late.refs_11_), channel_id=1, source_target_pairs={{0,1},{1,0},{2,4},{3,5},{4,2},{5,3},{6,8},{7,9},{8,6},{9,7},{10,12... | collective-permute-start | bytes 307208 | tf_op jit(solution)/shard_map/ppermute | solution.py:513
  6.3 5.1 %collective-permute-start = (bf16[1,80,128]{2,1,0:T(8,128)(2,1)S(1)}, bf16[1,80,128]{2,1,0:T(8,128)(2,1)S(1)}, u32[]{:S(2)}, u32[]{:S(2)}) collective-permute-start(bf16[1,80,128]{2,1,0:T(8,128)(2,1)S(1)} %get-tuple-element.95), channel_id=1, source_target_pairs={{0,2},{1,4},{2,0},{3,6},{4,1},{5,8},{6,3},{7,10},{8,5},{9,12},{10,... | collective-permute-start | bytes 61448 | tf_op jit(solution)/shard_map/ppermute | solution.py:513
  11.4 1.7 %copy-start.1 = (bf16[1,4,16,3072]{3,2,1,0:T(8,128)(2,1)S(1)}, bf16[1,4,16,3072]{3,2,1,0:T(8,128)(2,1)}, u32[]{:S(2)}) copy-start(bf16[1,4,16,3072]{3,2,1,0:T(8,128)(2,1)} %param.11) | copy-start | bytes 1179652
  11.4 1.7 %copy-start.3 = (s32[4,16,16]{2,1,0:T(8,128)S(1)}, s32[4,16,16]{2,1,0:T(8,128)}, u32[]{:S(2)}) copy-start(s32[4,16,16]{2,1,0:T(8,128)} %refs_2_.9) | copy-start | bytes 12292
  11.4 1.7 %copy-start.4 = (bf16[1,4,16,3072]{3,2,1,0:T(8,128)(2,1)S(1)}, bf16[1,4,16,3072]{3,2,1,0:T(8,128)(2,1)}, u32[]{:S(2)}) copy-start(bf16[1,4,16,3072]{3,2,1,0:T(8,128)(2,1)} %param.21) | copy-start | bytes 1179652
  11.4 1.6 %copy-start.5 = (f32[49,192]{1,0:T(8,128)S(1)}, f32[49,192]{1,0:T(8,128)}, u32[]{:S(2)}) copy-start(f32[49,192]{1,0:T(8,128)} %refs_4_.9) | copy-start | bytes 112900
  11.4 1.6 %copy-start.6 = (s32[4,8]{1,0:T(4,128)S(1)}, s32[4,8]{1,0:T(4,128)}, u32[]{:S(2)}) copy-start(s32[4,8]{1,0:T(4,128)} %refs_3_.9) | copy-start | bytes 388
  11.4 1.6 %copy-start.7 = (f32[192]{0:T(256)S(1)}, f32[192]{0:T(256)}, u32[]{:S(2)}) copy-start(f32[192]{0:T(256)} %param.15) | copy-start | bytes 2308
  11.5 1.6 %copy-start.8 = (f32[192]{0:T(256)S(1)}, f32[192]{0:T(256)}, u32[]{:S(2)}) copy-start(f32[192]{0:T(256)} %param.16) | copy-start | bytes 2308
  11.5 1.6 %copy-start.9 = (f32[192]{0:T(256)S(1)}, f32[192]{0:T(256)}, u32[]{:S(2)}) copy-start(f32[192]{0:T(256)} %param.20) | copy-start | bytes 2308
  11.5 1.6 %collective-permute-start.3 = (bf16[11,80,128]{2,1,0:T(8,128)(2,1)S(1)}, bf16[11,80,128]{2,1,0:T(8,128)(2,1)S(1)}, u32[]{:S(2)}, u32[]{:S(2)}) collective-permute-start(bf16[11,80,128]{2,1,0:T(8,128)(2,1)S(1)} %shard_map.179), channel_id=1, source_target_pairs={{0,1},{1,0},{2,3},{3,2},{4,5},{5,4},{6,7},{7,6},{8,9},{9,8},{10,11... | collective-permute-start | bytes 675848 | tf_op jit(solution)/shard_map/ppermute | solution.py:513
  28.6 1.6 %collective-permute-start.4 = (bf16[1216,128]{1,0:T(8,128)(2,1)S(1)}, bf16[1216,128]{1,0:T(8,128)(2,1)S(1)}, u32[]{:S(2)}, u32[]{:S(2)}) collective-permute-start(bf16[1216,128]{1,0:T(8,128)(2,1)S(1)} %get-tuple-element.101), channel_id=1, source_target_pairs={{0,1},{1,0},{2,3},{3,2},{4,5},{5,4},{6,7},{7,6},{8,9},{9,8},{10,11... | collective-permute-start | bytes 933896 | tf_op jit(solution)/shard_map/ppermute | solution.py:513
  30.4 6.4 %collective-permute-start.5 = (bf16[608,128]{1,0:T(8,128)(2,1)S(1)}, bf16[608,128]{1,0:T(8,128)(2,1)S(1)}, u32[]{:S(2)}, u32[]{:S(2)}) collective-permute-start(bf16[608,128]{1,0:T(8,128)(2,1)S(1)} %dynamic-slice_convert_fusion), channel_id=1, source_target_pairs={{0,64},{1,3},{2,66},{3,1},{4,68},{5,7},{6,70},{7,5},{8,72},{9,11},... | collective-permute-start | bytes 466952 | tf_op jit(solution)/shard_map/ppermute | solution.py:560
  31.4 5.4 %collective-permute-start.6 = (bf16[1,80,128]{2,1,0:T(8,128)(2,1)S(1)}, bf16[1,80,128]{2,1,0:T(8,128)(2,1)S(1)}, u32[]{:S(2)}, u32[]{:S(2)}) collective-permute-start(bf16[1,80,128]{2,1,0:T(8,128)(2,1)S(1)} %get-tuple-element.104), channel_id=1, source_target_pairs={{0,2},{1,4},{2,0},{3,6},{4,1},{5,8},{6,3},{7,10},{8,5},{9,12},{10,... | collective-permute-start | bytes 61448 | tf_op jit(solution)/shard_map/ppermute | solution.py:513
  35.1 5.0 %collective-permute-start.8 = (bf16[5,80,128]{2,1,0:T(8,128)(2,1)S(1)}, bf16[5,80,128]{2,1,0:T(8,128)(2,1)S(1)}, u32[]{:S(2)}, u32[]{:S(2)}) collective-permute-start(bf16[5,80,128]{2,1,0:T(8,128)(2,1)S(1)} %get-tuple-element.156.early.refs_5_), channel_id=1, source_target_pairs={{0,2},{1,3},{2,0},{3,1},{4,6},{5,7},{6,4},{7,5},{8,10},{9,11},{10,... | collective-permute-start | bytes 307208 | tf_op jit(solution)/shard_map/ppermute | solution.py:513
  36.8 5.2 %collective-permute-start.7 = (bf16[304,128]{1,0:T(8,128)(2,1)S(1)}, bf16[304,128]{1,0:T(8,128)(2,1)S(1)}, u32[]{:S(2)}, u32[]{:S(2)}) collective-permute-start(bf16[304,128]{1,0:T(8,128)(2,1)S(1)} %dynamic-slice_convert_fusion.1), channel_id=1, source_target_pairs={{0,192},{1,7},{2,194},{3,5},{4,196},{5,3},{6,198},{7,1},{8,200},{9... | collective-permute-start | bytes 233480 | tf_op jit(solution)/shard_map/ppermute | solution.py:560
  40.2 2.8 %collective-permute-start.10 = (bf16[5,80,128]{2,1,0:T(8,128)(2,1)S(1)}, bf16[5,80,128]{2,1,0:T(8,128)(2,1)S(1)}, u32[]{:S(2)}, u32[]{:S(2)}) collective-permute-start(bf16[5,80,128]{2,1,0:T(8,128)(2,1)S(1)} %get-tuple-element.157.late.refs_6_), channel_id=1, source_target_pairs={{0,1},{1,0},{2,4},{3,5},{4,2},{5,3},{6,8},{7,9},{8,6},{9,7},{10,12... | collective-permute-start | bytes 307208 | tf_op jit(solution)/shard_map/ppermute | solution.py:513
  42.0 3.2 %collective-permute-start.9 = (bf16[152,128]{1,0:T(8,128)(2,1)S(1)}, bf16[152,128]{1,0:T(8,128)(2,1)S(1)}, u32[]{:S(2)}, u32[]{:S(2)}) collective-permute-start(bf16[152,128]{1,0:T(8,128)(2,1)S(1)} %dynamic-slice_convert_fusion.2), channel_id=1, source_target_pairs={{0,2},{1,65},{2,0},{3,67},{4,6},{5,69},{6,4},{7,71},{8,10},{9,73},... | collective-permute-start | bytes 116744 | tf_op jit(solution)/shard_map/ppermute | solution.py:560
  45.3 5.8 %collective-permute-start.11 = (bf16[152,128]{1,0:T(8,128)(2,1)S(1)}, bf16[152,128]{1,0:T(8,128)(2,1)S(1)}, u32[]{:S(2)}, u32[]{:S(2)}) collective-permute-start(bf16[152,128]{1,0:T(8,128)(2,1)S(1)} %add_convert_fusion.4), channel_id=1, source_target_pairs={{0,6},{1,193},{2,4},{3,195},{4,2},{5,197},{6,0},{7,199},{8,14},{9,... | collective-permute-start | bytes 116744 | tf_op jit(solution)/shard_map/ppermute | solution.py:560
  47.5 6.6 %collective-permute-start.13 = (bf16[11,80,128]{2,1,0:T(8,128)(2,1)S(1)}, bf16[11,80,128]{2,1,0:T(8,128)(2,1)S(1)}, u32[]{:S(2)}, u32[]{:S(2)}) collective-permute-start(bf16[11,80,128]{2,1,0:T(8,128)(2,1)S(1)} %shard_map.181), channel_id=1, source_target_pairs={{0,1},{1,0},{2,3},{3,2},{4,5},{5,4},{6,7},{7,6},{8,9},{9,8},{10,11... | collective-permute-start | bytes 675848 | tf_op jit(solution)/shard_map/ppermute | solution.py:513
  51.1 2.9 %collective-permute-start.12 = (bf16[152,128]{1,0:T(8,128)(2,1)S(1)}, bf16[152,128]{1,0:T(8,128)(2,1)S(1)}, u32[]{:S(2)}, u32[]{:S(2)}) collective-permute-start(bf16[152,128]{1,0:T(8,128)(2,1)S(1)} %add_convert_fusion.3), channel_id=1, source_target_pairs={{0,8},{1,9},{2,10},{3,11},{4,12},{5,13},{6,14},{7,15},{8,0},{9,1},... | collective-permute-start | bytes 116744 | tf_op jit(solution)/shard_map/ppermute | solution.py:560
  54.0 9.7 %collective-permute-start.14 = (bf16[152,128]{1,0:T(8,128)(2,1)S(1)}, bf16[152,128]{1,0:T(8,128)(2,1)S(1)}, u32[]{:S(2)}, u32[]{:S(2)}) collective-permute-start(bf16[152,128]{1,0:T(8,128)(2,1)S(1)} %add_convert_fusion.2), channel_id=1, source_target_pairs={{0,24},{1,25},{2,26},{3,27},{4,28},{5,29},{6,30},{7,31},{8,16},{9,... | collective-permute-start | bytes 116744 | tf_op jit(solution)/shard_map/ppermute | solution.py:560
  63.8 4.3 %collective-permute-start.15 = (bf16[152,128]{1,0:T(8,128)(2,1)S(1)}, bf16[152,128]{1,0:T(8,128)(2,1)S(1)}, u32[]{:S(2)}, u32[]{:S(2)}) collective-permute-start(bf16[152,128]{1,0:T(8,128)(2,1)S(1)} %add_convert_fusion.1), channel_id=1, source_target_pairs={{0,56},{1,57},{2,58},{3,59},{4,60},{5,61},{6,62},{7,63},{8,48},{9,... | collective-permute-start | bytes 116744 | tf_op jit(solution)/shard_map/ppermute | solution.py:560
  68.0 3.1 %collective-permute-start.16 = (bf16[152,128]{1,0:T(8,128)(2,1)S(1)}, bf16[152,128]{1,0:T(8,128)(2,1)S(1)}, u32[]{:S(2)}, u32[]{:S(2)}) collective-permute-start(bf16[152,128]{1,0:T(8,128)(2,1)S(1)} %add_convert_fusion), channel_id=1, source_target_pairs={{0,2},{1,65},{2,0},{3,67},{4,6},{5,69},{6,4},{7,71},{8,10},{9,73},... | collective-permute-start | bytes 116744 | tf_op jit(solution)/shard_map/ppermute | solution.py:560
  71.2 4.5 %collective-permute-start.17 = (bf16[304,128]{1,0:T(8,128)(2,1)S(1)}, bf16[304,128]{1,0:T(8,128)(2,1)S(1)}, u32[]{:S(2)}, u32[]{:S(2)}) collective-permute-start(bf16[304,128]{1,0:T(8,128)(2,1)S(1)} %maximum_select_fusion.3), channel_id=1, source_target_pairs={{0,192},{1,7},{2,194},{3,5},{4,196},{5,3},{6,198},{7,1},{8,200},{9... | collective-permute-start | bytes 233480 | tf_op jit(solution)/shard_map/ppermute | solution.py:560
  75.8 4.2 %collective-permute-start.18 = (bf16[608,128]{1,0:T(8,128)(2,1)S(1)}, bf16[608,128]{1,0:T(8,128)(2,1)S(1)}, u32[]{:S(2)}, u32[]{:S(2)}) collective-permute-start(bf16[608,128]{1,0:T(8,128)(2,1)S(1)} %maximum_select_fusion.2), channel_id=1, source_target_pairs={{0,64},{1,3},{2,66},{3,1},{4,68},{5,7},{6,70},{7,5},{8,72},{9,11},... | collective-permute-start | bytes 466952 | tf_op jit(solution)/shard_map/ppermute | solution.py:560
  80.1 10.6 %collective-permute-start.19 = (bf16[1216,128]{1,0:T(8,128)(2,1)S(1)}, bf16[1216,128]{1,0:T(8,128)(2,1)S(1)}, u32[]{:S(2)}, u32[]{:S(2)}) collective-permute-start(bf16[1216,128]{1,0:T(8,128)(2,1)S(1)} %maximum_select_fusion.1), channel_id=1, source_target_pairs={{0,1},{1,0},{2,3},{3,2},{4,5},{5,4},{6,7},{7,6},{8,9},{9,8},{10,11... | collective-permute-start | bytes 933896 | tf_op jit(solution)/shard_map/ppermute | solution.py:513
  (1 other events, 0.8 us)
